TPU v7x, 32 devices: a whole 2x2x4 slice. The times are simulated.
32 devices in a mesh: expert: 8 (over y, x, core), dp: 4 (over z).
Axes of the slice: x: 2, y: 2, z: 4, core: 2. Of those that a mesh axis runs over, the one named last changes fastest.
Arguments:
- tokens: bfloat16 [4, 4096, 2048], P('dp', 'expert'), may hold values from -6 to 6
- cotangent: bfloat16 [4, 4096, 2048], P('dp', 'expert'), may hold values from -0.13183594 to 0.13183594
- routes: int32 [4, 4096, 1], P('dp', 'expert'), may hold values from 0 to 7; in each aligned block of 512 rows (0 to 511, 512 to 1023, ..., all dimensions but the last counted through in order) at most 128 rows name the same one
- owner: int32 [8], replicated, may hold values from 0 to 7, as said below
- master: float32 [8, 2048, 2304], P('expert', 'dp'), may hold values from -0.125 to 0.125
- moment1: float32 [8, 2048, 2304], P('expert', 'dp'), may hold values from -1.8 to 1.8
- moment2: float32 [8, 2048, 2304], P('expert', 'dp'), may hold values from 0.01 to 1
Outputs:
- token_grad: bfloat16 [4, 4096, 2048], P('dp', 'expert')
- new_master: float32 [8, 2048, 2304], P('expert', 'dp')
- new_moment1: float32 [8, 2048, 2304], P('expert', 'dp')
- new_moment2: float32 [8, 2048, 2304], P('expert', 'dp')
Inputs may be any that keep to these rules, and one draw needn't show every extreme that they name: owner[j] is j or j xor (4), and owner[j] == j exactly when the same holds for j xor (4); at least one pair moves. `routes`: among the 512 tokens of one device at most 128 choose one expert, and some expert is chosen by exactly 128.
All inputs are finite; a program needn't handle non-finite values.
Results may differ from a plain program's by a relative error of at most 0.012.
Values may be sent and summed in bfloat16 or wider, within the bound.
A program may use at most 128 MiB of HBM per device.

v0:
```python
import jax
import jax.numpy as jnp
from jax import lax
from jax.sharding import PartitionSpec as P


def swapped(value, axis, apart):
    return lax.ppermute(value, axis, [(i, i ^ 1 << apart) for i in range(lax.axis_size(axis))])


def per_device(tokens, cotangent, routes, owner, master, moment1, moment2):
    experts = lax.axis_size("expert")
    bit = experts.bit_length() - 2
    position = lax.axis_index("expert")
    keep = owner[position] == position
    hidden_units = master.shape[2] // 3
    partner = (
        swapped(master.astype(jnp.bfloat16), "expert", bit).astype(master.dtype),
        swapped(moment1.astype(jnp.bfloat16), "expert", bit).astype(moment1.dtype),
        swapped(moment2.astype(jnp.bfloat16), "expert", bit).astype(moment2.dtype),
    )
    placed_master = jnp.where(keep, master, partner[0])
    placed_first = jnp.where(keep, moment1, partner[1])
    placed_second = jnp.where(keep, moment2, partner[2])
    weights = lax.all_gather(placed_master[0].astype(jnp.bfloat16), "dp", axis=0, tiled=True)
    features = weights.shape[0]
    tok_count = tokens.shape[1]
    capacity = 2 * tok_count // experts
    route_ids = routes[0, :, 0]
    columns = jnp.arange(experts, dtype=jnp.int32)
    onehot = (route_ids[:, None] == columns[None, :]).astype(jnp.int32)
    slot = jnp.sum((jnp.cumsum(onehot, axis=0) - 1) * onehot, axis=1)
    flat = route_ids * capacity + slot
    send_x = jnp.zeros((experts * capacity, features), jnp.bfloat16).at[flat].set(tokens[0])
    send_dy = jnp.zeros((experts * capacity, features), jnp.bfloat16).at[flat].set(cotangent[0])
    gate_up = weights[:, : 2 * hidden_units]
    down = weights[:, 2 * hidden_units :]
    got_x, got_dy = (
        lax.all_to_all(
            send_x.reshape(experts, capacity, features),
            "expert",
            split_axis=0,
            concat_axis=0,
            tiled=True,
        ),
        lax.all_to_all(
            send_dy.reshape(experts, capacity, features),
            "expert",
            split_axis=0,
            concat_axis=0,
            tiled=True,
        ),
    )
    rows_x = got_x.reshape(experts * capacity, features)
    rows_dy = got_dy.reshape(experts * capacity, features)
    pre = jnp.dot(rows_x, gate_up, preferred_element_type=jnp.float32)
    gate_pre = pre[:, :hidden_units]
    up_pre = pre[:, hidden_units:]
    sig = jax.nn.sigmoid(gate_pre)
    act = gate_pre * sig
    hidden = (act * up_pre).astype(jnp.bfloat16)
    d_hidden = jnp.dot(rows_dy, down, preferred_element_type=jnp.float32)
    d_gate = (d_hidden * up_pre * sig * (1.0 + gate_pre * (1.0 - sig))).astype(jnp.bfloat16)
    d_up = (d_hidden * act).astype(jnp.bfloat16)
    d_both = jnp.concatenate([d_gate, d_up], axis=1)
    left = jnp.einsum("rd,rk->dk", rows_x, d_both, preferred_element_type=jnp.float32)
    right = jnp.einsum("rd,rk->dk", rows_dy, hidden, preferred_element_type=jnp.float32)
    grad = lax.psum_scatter(
        jnp.concatenate([left, right], axis=1).astype(jnp.bfloat16),
        "dp",
        scatter_dimension=0,
        tiled=True,
    ).astype(jnp.float32)
    in_grad = jnp.einsum("rk,dk->rd", d_both, gate_up, preferred_element_type=jnp.float32).astype(
        jnp.bfloat16
    )
    returned = lax.all_to_all(
        in_grad.reshape(experts, capacity, features),
        "expert",
        split_axis=0,
        concat_axis=0,
        tiled=True,
    )
    token_grad = returned.reshape(experts * capacity, features)[flat]
    new_first = 0.9 * placed_first[0] + 0.1 * grad
    new_second = 0.95 * placed_second[0] + 0.05 * grad * grad
    update = new_first / (1.0 - 0.9**10) / (jnp.sqrt(new_second / (1.0 - 0.95**10)) + 1e-08)
    new_master = placed_master[0] - 0.003 * (update + 0.1 * placed_master[0])
    return (token_grad[None], new_master[None], new_first[None], new_second[None])


def solution(mesh):
    placed = (
        P("dp", "expert", None),
        P("dp", "expert", None),
        P("dp", "expert", None),
        P(),
        P("expert", "dp", None),
        P("expert", "dp", None),
        P("expert", "dp", None),
    )
    return jax.shard_map(
        per_device,
        mesh=mesh,
        in_specs=placed,
        out_specs=(
            P("dp", "expert", None),
            P("expert", "dp", None),
            P("expert", "dp", None),
            P("expert", "dp", None),
        ),
        check_vma=False,
    )
```

profile of v0, /device:TPU:0, one launch (start us, length us, event | category | flops | bytes accessed | tf_op | source)
XLA Modules:
  0.0 505.9 jit_solution(17217411266020198612)
XLA Ops:
  7.2 6.2 %copy.23 = f32[1,512,2304]{1,2,0:T(8,128)} copy(f32[1,512,2304]{2,1,0:T(8,128)} %param.11) | data formatting | bytes 9437184 | tf_op args[4]
  13.4 4.1 convert_element_type.43
  17.5 3.0 collective-permute-start
  21.7 50.3 %collective-permute-done = bf16[1,512,2304]{1,2,0:T(8,128)(2,1)} collective-permute-done((bf16[1,512,2304]{1,2,0:T(8,128)(2,1)}, bf16[1,512,2304]{1,2,0:T(8,128)(2,1)}, u32[]{:S(2)}, u32[]{:S(2)}) %collective-permute-start) | collective-permute-done | bytes 2359328 | tf_op jit(solution)/shard_map/ppermute | solution.py:8
  72.0 3.9 bitcast_convert_fusion
  76.0 1.1 reduce-window.6
  77.5 6.3 %scatter_custom_fusion.1 = bf16[1024,2048]{1,0:T(8,128)(2,1)} fusion(s32[512]{0:T(512)S(1)} %bitcast.68, bf16[1,512,2048]{2,1,0:T(8,128)(2,1)S(1)} %copy-done, bf16[]{:T(256)} %constant.17.clone.1), kind=kCustom, calls=%fused_computation.30 | custom fusion | bytes 6291458 | tf_op jit(solution)/shard_map/scatter | solution.py:34
  83.7 4.9 all-to-all-start.1
  88.7 6.5 %scatter_custom_fusion = bf16[1024,2048]{1,0:T(8,128)(2,1)} fusion(s32[512]{0:T(512)S(1)} %bitcast.69, bf16[1,512,2048]{2,1,0:T(8,128)(2,1)S(1)} %copy-done.2, bf16[]{:T(256)} %constant.17.clone.1), kind=kCustom, calls=%fused_computation.32 | custom fusion | bytes 6291458 | tf_op jit(solution)/shard_map/scatter | solution.py:35
  95.2 42.6 %all-to-all-done.1 = bf16[8,128,2048]{2,1,0:T(8,128)(2,1)} async-done(((bf16[8,128,2048]{2,1,0:T(8,128)(2,1)}), bf16[8,128,2048]{2,1,0:T(8,128)(2,1)}, u32[]{:S(2)}, u32[]{:S(2)}) %all-to-all-start.1) | async-done | bytes 4194336 | tf_op jit(solution)/shard_map/all_to_all | solution.py:39
  137.8 4.5 all-to-all-start
  142.4 102.0 %all-gather.2.cloned.1.call-done = bf16[2048,2304]{0,1:T(8,128)(2,1)} async-done(((bf16[512,2304]{0,1:T(8,128)(2,1)}), bf16[2048,2304]{0,1:T(8,128)(2,1)}) %all-gather.2.cloned.1.call-update) | async-done | bytes 9437200 | tf_op jit(solution)/shard_map/all_gather | solution.py:25
  244.3 11.7 %fusion.2 = f32[1024,1536]{0,1:T(8,128)} fusion(bf16[1024,2048]{1,0:T(8,128)(2,1)} %bitcast.14, bf16[2048,2304]{0,1:T(8,128)(2,1)} %all-gather.2.cloned.1.call-done), kind=kOutput, calls=%fused_computation.9 | convolution fusion | flops 6442450944 | bytes 16777216 | tf_op jit(solution)/shard_map/dot_general | solution.py:56
  256.1 7.6 %convolution_convert_fusion.1 = bf16[2048,768]{0,1:T(8,128)(2,1)S(1)} fusion(bf16[1024,2048]{1,0:T(8,128)(2,1)} %bitcast.9, f32[1024,1536]{0,1:T(8,128)} %fusion.2), kind=kOutput, calls=%fused_computation.21 | convolution fusion | flops 3227516928 | bytes 13631488 | tf_op jit(solution)/shard_map/rd,rk->dk/dot_general | solution.py:67
  263.8 7.5 %multiply_convert_fusion.2 = (bf16[1024,768]{0,1:T(8,128)(2,1)S(1)}, bf16[1024,768]{0,1:T(8,128)(2,1)S(1)}) fusion(f32[1024,1536]{0,1:T(8,128)S(1)} %copy-done.5, bf16[1024,2048]{1,0:T(8,128)(2,1)} %bitcast.9, bf16[2048,2304]{0,1:T(8,128)(2,1)} %all-gather.2.cloned.1.call-done), kind=kOutput, calls=%fused_computation.27 | convolution fusion | flops 3231449088 | bytes 16777216 | tf_op jit(solution)/shard_map/dot_general | solution.py:62
  271.3 11.1 %convolution_convert_fusion = bf16[2048,1536]{0,1:T(8,128)(2,1)S(1)} fusion(bf16[1024,2048]{1,0:T(8,128)(2,1)} %bitcast.14, bf16[1024,768]{0,1:T(8,128)(2,1)S(1)} %get-tuple-element.16, bf16[1024,768]{0,1:T(8,128)(2,1)S(1)} %get-tuple-element.15), kind=kOutput, calls=%fused_computation.4 | convolution fusion | flops 6451888128 | bytes 13631488 | tf_op jit(solution)/shard_map/rd,rk->dk/dot_general | solution.py:66
  282.4 21.5 %pad_maximum_fusion = bf16[2048,2304]{0,1:T(8,128)(2,1)} fusion(bf16[2048,768]{0,1:T(8,128)(2,1)S(1)} %convolution_convert_fusion.1, bf16[2048,1536]{0,1:T(8,128)(2,1)S(1)} %convolution_convert_fusion), kind=kLoop, calls=%fused_computation.3 | loop fusion | flops 18874368 | bytes 18874368 | tf_op jit(solution)/shard_map/concatenate | solution.py:69
  304.0 10.8 %fusion.9 = bf16[1024,2048]{1,0:T(8,128)(2,1)} fusion(bf16[2048,2304]{0,1:T(8,128)(2,1)} %all-gather.2.cloned.1.call-done, bf16[1024,768]{0,1:T(8,128)(2,1)} %copy-done.6, bf16[1024,768]{0,1:T(8,128)(2,1)S(1)} %get-tuple-element.15), kind=kOutput, calls=%fused_computation.20 | convolution fusion | flops 6450839552 | bytes 13631488 | tf_op jit(solution)/shard_map/rk,dk->rd/dot_general | solution.py:74
  314.8 4.5 all-to-all-start.2
  319.3 6.0 %copy.29 = f32[1,512,2304]{1,2,0:T(8,128)} copy(f32[1,512,2304]{2,1,0:T(8,128)} %param.13) | data formatting | bytes 9437184 | tf_op args[6]
  325.4 4.1 convert_element_type.53
  329.5 1.9 collective-permute-start.2
  331.4 6.0 %copy.27 = f32[1,512,2304]{1,2,0:T(8,128)} copy(f32[1,512,2304]{2,1,0:T(8,128)} %param.12) | data formatting | bytes 9437184 | tf_op args[5]
  337.5 4.0 convert_element_type.49
  341.7 26.8 %all-to-all-done.2 = bf16[8,128,2048]{2,1,0:T(8,128)(2,1)} async-done(((bf16[8,128,2048]{2,1,0:T(8,128)(2,1)}), bf16[8,128,2048]{2,1,0:T(8,128)(2,1)}, u32[]{:S(2)}, u32[]{:S(2)}) %all-to-all-start.2) | async-done | bytes 4194336 | tf_op jit(solution)/shard_map/all_to_all | solution.py:77
  368.6 8.1 %gather_fusion = bf16[512,2048]{1,0:T(8,128)(2,1)} fusion(bf16[1024,2048]{1,0:T(8,128)(2,1)} %bitcast.16, s32[1024]{0:T(1024)S(1)} %pad_clamp_fusion), kind=kCustom, calls=%fused_computation | custom fusion | bytes 4196352 | tf_op jit(solution)/shard_map/gather | solution.py:84
  376.6 41.9 %collective-permute-done.2 = bf16[1,512,2304]{1,2,0:T(8,128)(2,1)} collective-permute-done((bf16[1,512,2304]{1,2,0:T(8,128)(2,1)}, bf16[1,512,2304]{1,2,0:T(8,128)(2,1)}, u32[]{:S(2)}, u32[]{:S(2)}) %collective-permute-start.2) | collective-permute-done | bytes 2359328 | tf_op jit(solution)/shard_map/ppermute | solution.py:8
  418.5 50.1 %collective-permute-done.1 = bf16[1,512,2304]{1,2,0:T(8,128)(2,1)} collective-permute-done((bf16[1,512,2304]{1,2,0:T(8,128)(2,1)}, bf16[1,512,2304]{1,2,0:T(8,128)(2,1)}, u32[]{:S(2)}, u32[]{:S(2)}) %collective-permute-start.1) | collective-permute-done | bytes 2359328 | tf_op jit(solution)/shard_map/ppermute | solution.py:8
  468.6 11.9 %fusion.22 = (f32[1,512,2304]{1,2,0:T(8,128)}, f32[1,512,2304]{1,2,0:T(8,128)}, f32[1,512,2304]{1,2,0:T(8,128)}) fusion(bf16[512,2304]{0,1:T(8,128)(2,1)} %reduce-scatter.2.cloned.1.call-done, f32[1,512,2304]{1,2,0:T(8,128)} %copy.29, bf16[1,512,2304]{1,2,0:T(8,128)(2,1)} %collective-permute-done.2, pred[]{:T(512)S(6)} %eq.36, f32[1,512,2304]{1,2,0:T(8,128)} %copy.27, ...), kind=kLoop, calls=%fused_computation.37 | loop fusion | flops 25952256 | bytes 37748736 | tf_op jit(solution)/shard_map/broadcast_in_dim | solution.py:89
  480.6 6.0 %copy.30 = f32[1,512,2304]{2,1,0:T(8,128)} copy(f32[1,512,2304]{1,2,0:T(8,128)} %get-tuple-element.13) | data formatting | bytes 9437184
  486.6 6.0 %copy.31 = f32[1,512,2304]{2,1,0:T(8,128)} copy(f32[1,512,2304]{1,2,0:T(8,128)} %get-tuple-element.14) | data formatting | bytes 9437184
  492.6 6.2 %copy.32 = f32[1,512,2304]{2,1,0:T(8,128)} copy(f32[1,512,2304]{1,2,0:T(8,128)} %get-tuple-element.12) | data formatting | bytes 9437184
  (29 shorter events, 1.3 us)
Async XLA Ops:
  7.2 70.3 %copy-start = (bf16[1,512,2048]{2,1,0:T(8,128)(2,1)S(1)}, bf16[1,512,2048]{2,1,0:T(8,128)(2,1)}, u32[]{:S(2)}) copy-start(bf16[1,512,2048]{2,1,0:T(8,128)(2,1)} %param.7) | copy-start | bytes 6291460
  7.2 237.2 %all-gather.2.cloned.1.call-start = ((), (), s32[]{:S(2)}) async-start(), calls=%async_computation.4 | async-start | bytes 11796480 | tf_op jit(solution)/shard_map/all_gather | solution.py:25
  13.4 7.0 %copy-start.4 = (s32[8]{0:T(128)S(1)}, s32[8]{0:T(128)}, u32[]{:S(2)}) copy-start(s32[8]{0:T(128)} %param.10) | copy-start | bytes 100
  17.5 54.5 %collective-permute-start = (bf16[1,512,2304]{1,2,0:T(8,128)(2,1)}, bf16[1,512,2304]{1,2,0:T(8,128)(2,1)}, u32[]{:S(2)}, u32[]{:S(2)}) collective-permute-start(bf16[1,512,2304]{1,2,0:T(8,128)(2,1)} %convert_element_type.43), channel_id=1, source_target_pairs={{0,16},{4,20},{8,24},{12,28},{16,0},{20,4},{24,8},{28,12},{1,17},{... | collective-permute-start | bytes 7077896 | tf_op jit(solution)/shard_map/ppermute | solution.py:8
  21.7 54.3 %copy-start.3 = (s32[1,512,1]{1,2,0:T(1,128)S(1)}, s32[1,512,1]{1,2,0:T(1,128)}, u32[]{:S(2)}) copy-start(s32[1,512,1]{1,2,0:T(1,128)} %param.9) | copy-start | bytes 6148
  83.7 4.9 copy-start.2
  83.7 54.0 %all-to-all-start.1 = ((bf16[8,128,2048]{2,1,0:T(8,128)(2,1)}), bf16[8,128,2048]{2,1,0:T(8,128)(2,1)}, u32[]{:S(2)}, u32[]{:S(2)}) async-start(bf16[8,128,2048]{2,1,0:T(8,128)(2,1)} %bitcast.63), calls=%async_computation.1 | async-start | bytes 8388608 | tf_op jit(solution)/shard_map/all_to_all | solution.py:39
  137.8 118.3 %all-to-all-start = ((bf16[8,128,2048]{2,1,0:T(8,128)(2,1)}), bf16[8,128,2048]{2,1,0:T(8,128)(2,1)}, u32[]{:S(2)}, u32[]{:S(2)}) async-start(bf16[8,128,2048]{2,1,0:T(8,128)(2,1)} %bitcast.62), calls=%async_computation | async-start | bytes 8388608 | tf_op jit(solution)/shard_map/all_to_all | solution.py:46
  142.3 326.3 %reduce-scatter.2.cloned.1.call-start = ((), (), s32[]{:S(2)}) async-start(), calls=%async_computation.5 | async-start | bytes 11796480 | tf_op jit(solution)/shard_map/reduce_scatter | solution.py:68
  256.1 7.7 %copy-start.5 = (f32[1024,1536]{0,1:T(8,128)S(1)}, f32[1024,1536]{0,1:T(8,128)}, u32[]{:S(2)}) copy-start(f32[1024,1536]{0,1:T(8,128)} %fusion.2) | copy-start | bytes 18874372
  271.3 11.1 %copy-start.6 = (bf16[1024,768]{0,1:T(8,128)(2,1)}, bf16[1024,768]{0,1:T(8,128)(2,1)S(1)}, u32[]{:S(2)}) copy-start(bf16[1024,768]{0,1:T(8,128)(2,1)S(1)} %get-tuple-element.16) | copy-start | bytes 4718596
  314.8 53.8 %all-to-all-start.2 = ((bf16[8,128,2048]{2,1,0:T(8,128)(2,1)}), bf16[8,128,2048]{2,1,0:T(8,128)(2,1)}, u32[]{:S(2)}, u32[]{:S(2)}) async-start(bf16[8,128,2048]{2,1,0:T(8,128)(2,1)} %bitcast.64), calls=%async_computation.2 | async-start | bytes 8388608 | tf_op jit(solution)/shard_map/all_to_all | solution.py:77
  329.5 89.0 %collective-permute-start.2 = (bf16[1,512,2304]{1,2,0:T(8,128)(2,1)}, bf16[1,512,2304]{1,2,0:T(8,128)(2,1)}, u32[]{:S(2)}, u32[]{:S(2)}) collective-permute-start(bf16[1,512,2304]{1,2,0:T(8,128)(2,1)} %convert_element_type.53), channel_id=1, source_target_pairs={{0,16},{4,20},{8,24},{12,28},{16,0},{20,4},{24,8},{28,12},{1,17},{... | collective-permute-start | bytes 7077896 | tf_op jit(solution)/shard_map/ppermute | solution.py:8
  341.5 127.1 %collective-permute-start.1 = (bf16[1,512,2304]{1,2,0:T(8,128)(2,1)}, bf16[1,512,2304]{1,2,0:T(8,128)(2,1)}, u32[]{:S(2)}, u32[]{:S(2)}) collective-permute-start(bf16[1,512,2304]{1,2,0:T(8,128)(2,1)} %convert_element_type.49), channel_id=1, source_target_pairs={{0,16},{4,20},{8,24},{12,28},{16,0},{20,4},{24,8},{28,12},{1,17},{... | collective-permute-start | bytes 7077896 | tf_op jit(solution)/shard_map/ppermute | solution.py:8
  492.6 6.2 %copy-start.1 = (bf16[1,512,2048]{2,1,0:T(8,128)(2,1)S(1)}, bf16[1,512,2048]{2,1,0:T(8,128)(2,1)}, u32[]{:S(2)}) copy-start(bf16[1,512,2048]{2,1,0:T(8,128)(2,1)} %param.7) | copy-start | bytes 6291460
Sparse Core Ops, SparseCore 0:
  76.1 168.2 all-gather.1
  304.1 159.4 reduce-scatter.1
where the time goes:
time: 511 us; the launch traced here: 506 us
  waiting for transfers between devices  314 us (61%)
  local copies, waits for them, and re-layouts  58.2 us (11%)
  other arithmetic  50.9 us (10%)
  matrix products  48.8 us (10%)
  starting transfers between devices  19.1 us (4%)
  between operations  15 us (3%)
    ppermute x3, waiting for transfers between devices, swapped(): lax.ppermute(value, axis, [(i, i ^ 1 << apart) for i in range(lax.axis_si...  142 us
    all_gather x1, waiting for transfers between devices, per_device(): lax.all_gather(placed_master[0].astype(jnp.bfloat16), 'dp', axis=0, tiled...  102 us
    all_to_all x1, waiting for transfers between devices, per_device(): lax.all_to_all(send_x.reshape(experts, capacity, features), 'expert', spl...  42.6 us
    unnamed x20, local copies, waits for them, and re-layouts  36.6 us
    all_to_all x1, waiting for transfers between devices, per_device(): lax.all_to_all(in_grad.reshape(experts, capacity, features), 'expert', sp...  26.8 us
    concatenate x1, other arithmetic, per_device(): jnp.concatenate([left, right], axis=1).astype(jnp.bfloat16)  21.5 us
    scatter x2, local copies, waits for them, and re-layouts, per_device(): jnp.zeros((experts * capacity, features), jnp.bfloat16).at[flat]  12.8 us
    broadcast_in_dim x1, other arithmetic, per_device(): new_second[None]  11.9 us
  transfers between devices with their start and end apart: 8, of which 6 were waited for; matrix products, arithmetic and copies ran while one was open for 13% of the time, Pallas kernels for 0%

commit v1 on v0

v1 whole, which is shorter than its diff:
```python
import functools

import jax
import jax.numpy as jnp
from jax import lax
from jax.experimental import pallas as pl
from jax.experimental.pallas import tpu as pltpu
from jax.sharding import PartitionSpec as P

CHUNKS = 3
BF = jnp.bfloat16
F32 = jnp.float32


def swapped(value, apart):
    size = lax.axis_size("expert")
    return lax.ppermute(value, "expert", [(i, i ^ 1 << apart) for i in range(size)])


def pack_body(gate, up, down, out):
    width = gate.shape[1]
    out[:, :width] = gate[...].astype(BF)
    out[:, width : 2 * width] = up[...].astype(BF)
    out[:, 2 * width :] = down[...].astype(BF)


def pack(master, chunk):
    rows, columns = master.shape
    width = columns // (3 * CHUNKS)
    tile = min(rows, 128)
    return pl.pallas_call(
        pack_body,
        grid=(rows // tile,),
        in_specs=[
            pl.BlockSpec((tile, width), functools.partial(lambda c, i: (i, c), part * CHUNKS + chunk))
            for part in range(3)
        ],
        out_specs=pl.BlockSpec((tile, 3 * width), lambda i: (i, 0)),
        out_shape=jax.ShapeDtypeStruct((rows, 3 * width), BF),
        cost_estimate=pl.CostEstimate(flops=0, bytes_accessed=6 * rows * 3 * width, transcendentals=0),
    )(master, master, master)


def narrow_body(source, out):
    out[...] = source[...].astype(BF)


def narrow(state):
    rows, columns = state.shape
    tile = min(rows, 128)
    return pl.pallas_call(
        narrow_body,
        grid=(rows // tile,),
        in_specs=[pl.BlockSpec((tile, columns), lambda i: (i, 0))],
        out_specs=pl.BlockSpec((tile, columns), lambda i: (i, 0)),
        out_shape=jax.ShapeDtypeStruct((rows, columns), BF),
        cost_estimate=pl.CostEstimate(flops=0, bytes_accessed=6 * rows * columns, transcendentals=0),
    )(state)


def update_body(keep, master, first, second, other_master, other_first, other_second, grad, *rest):
    new_master, new_first, new_second = rest[-3:]
    stay = keep[0] == 1
    placed = jnp.where(stay, master[...], other_master[...].astype(F32))
    m1 = jnp.where(stay, first[...], other_first[...].astype(F32))
    m2 = jnp.where(stay, second[...], other_second[...].astype(F32))
    g = grad[...].astype(F32)
    m1 = 0.9 * m1 + 0.1 * g
    m2 = 0.95 * m2 + 0.05 * g * g
    step = m1 / (1.0 - 0.9**10) / (jnp.sqrt(m2 / (1.0 - 0.95**10)) + 1e-08)
    new_first[...] = m1
    new_second[...] = m2
    new_master[...] = placed - 0.003 * (step + 0.1 * placed)


def update(keep, states, others, grad, chunk, before):
    rows, columns = states[0].shape
    width = columns // (3 * CHUNKS)
    tile = min(rows, 256)
    wide = pl.BlockSpec((tile, width), lambda part, i: (i, part * CHUNKS + chunk))
    near = pl.BlockSpec((tile, width), lambda part, i: (i, part))
    count = 0 if before is None else 3
    return pl.pallas_call(
        update_body,
        grid=(3, rows // tile),
        in_specs=[pl.BlockSpec(memory_space=pltpu.SMEM)]
        + [wide] * 3
        + [near, wide, wide, near]
        + [pl.BlockSpec(memory_space=pl.ANY)] * count,
        out_specs=[wide] * 3,
        out_shape=[jax.ShapeDtypeStruct((rows, columns), F32)] * 3,
        input_output_aliases={8 + i: i for i in range(count)},
        cost_estimate=pl.CostEstimate(
            flops=20 * rows * 3 * width, bytes_accessed=32 * rows * 3 * width, transcendentals=0
        ),
    )(keep, *states, *others, grad, *(before or ()))


def after(value, *earlier):
    return lax.optimization_barrier((value, *earlier))[0]


def per_device(tokens, cotangent, routes, owner, master, moment1, moment2):
    experts = lax.axis_size("expert")
    bit = experts.bit_length() - 2
    position = lax.axis_index("expert")
    keep = owner[position] == position
    flag = keep.astype(jnp.int32).reshape(1)
    states = (master[0], moment1[0], moment2[0])
    width = master.shape[2] // (3 * CHUNKS)
    tok_count = tokens.shape[1]
    capacity = 2 * tok_count // experts
    slots = experts * capacity
    features = tokens.shape[2]

    packed = [pack(states[0], c) for c in range(CHUNKS)]
    route_ids = routes[0, :, 0]
    columns = jnp.arange(experts, dtype=jnp.int32)
    onehot = (route_ids[:, None] == columns[None, :]).astype(jnp.int32)
    slot = jnp.sum((jnp.cumsum(onehot, axis=0) - 1) * onehot, axis=1)
    flat = route_ids * capacity + slot
    place = (jnp.arange(slots, dtype=jnp.int32)[:, None] == flat[None, :]).astype(BF)
    take = (flat[:, None] == jnp.arange(slots, dtype=jnp.int32)[None, :]).astype(BF)

    def exchange(rows):
        return lax.all_to_all(
            rows.reshape(experts, capacity, features), "expert", split_axis=0, concat_axis=0, tiled=True
        ).reshape(slots, features)

    send_x = jnp.dot(place, tokens[0], preferred_element_type=F32).astype(BF)
    send_dy = jnp.dot(place, cotangent[0], preferred_element_type=F32).astype(BF)

    def gathered(chunk, partner):
        placed = jnp.where(keep, packed[chunk], partner)
        return lax.all_gather(placed, "dp", axis=0, tiled=True)

    other = [None] * CHUNKS
    weights = [None] * CHUNKS
    other[0] = swapped(packed[0], bit)
    weights[0] = gathered(0, other[0])
    rows_x = exchange(after(send_x, other[0]))
    other[1] = swapped(after(packed[1], other[0]), bit)
    weights[1] = gathered(1, other[1])
    rows_dy = exchange(after(send_dy, rows_x))
    other[2] = swapped(after(packed[2], rows_x), bit)
    weights[2] = gathered(2, other[2])
    narrow_first = narrow(states[1])
    narrow_second = narrow(states[2])
    other_first = swapped(after(narrow_first, rows_dy), bit)
    other_second = swapped(after(narrow_second, other_first), bit)

    total = None
    grads = []
    for c in range(CHUNKS):
        gate_up = weights[c][:, : 2 * width]
        down = weights[c][:, 2 * width :]
        pre = jnp.dot(rows_x, gate_up, preferred_element_type=F32)
        gate_pre = pre[:, :width]
        up_pre = pre[:, width:]
        sig = jax.nn.sigmoid(gate_pre)
        act = gate_pre * sig
        hidden = (act * up_pre).astype(BF)
        d_hidden = jnp.dot(rows_dy, down, preferred_element_type=F32)
        d_gate = (d_hidden * up_pre * sig * (1.0 + gate_pre * (1.0 - sig))).astype(BF)
        d_up = (d_hidden * act).astype(BF)
        d_both = jnp.concatenate([d_gate, d_up], axis=1)
        left = jnp.einsum("rd,rk->dk", rows_x, d_both, preferred_element_type=F32)
        right = jnp.einsum("rd,rk->dk", rows_dy, hidden, preferred_element_type=F32)
        grads.append(
            lax.psum_scatter(
                jnp.concatenate([left.astype(BF), right.astype(BF)], axis=1),
                "dp",
                scatter_dimension=0,
                tiled=True,
            )
        )
        part = jnp.einsum("rk,dk->rd", d_both, gate_up, preferred_element_type=F32)
        total = part if total is None else total + part
    returned = exchange(total.astype(BF))
    token_grad = jnp.dot(take, returned, preferred_element_type=F32).astype(BF)

    made = None
    for c in range(CHUNKS):
        made = update(flag, states, (other[c], other_first, other_second), grads[c], c, made)
    return (token_grad[None], made[0][None], made[1][None], made[2][None])


def solution(mesh):
    placed = (
        P("dp", "expert", None),
        P("dp", "expert", None),
        P("dp", "expert", None),
        P(),
        P("expert", "dp", None),
        P("expert", "dp", None),
        P("expert", "dp", None),
    )
    return jax.shard_map(
        per_device,
        mesh=mesh,
        in_specs=placed,
        out_specs=(
            P("dp", "expert", None),
            P("expert", "dp", None),
            P("expert", "dp", None),
            P("expert", "dp", None),
        ),
        check_vma=False,
    )
```

time: 511 us -> 433 us (0.85)
  waiting for transfers between devices: 314 us -> 247 us
  local copies, waits for them, and re-layouts: 58.2 us -> 2.85 us
  other arithmetic: 50.9 us -> 10.1 us
  Pallas kernels: 0 us -> 40.4 us
  matrix products: 48.8 us -> 86.6 us
    all_gather x1 -> x3, waiting for transfers between devices: 102 us -> 15.9 us  [gathered(): return lax.all_gather(placed, 'dp', axis=0, tiled=True)]
    ppermute x3 -> x5, waiting for transfers between devices: 142 us -> 79.9 us  [swapped(): lax.ppermute(value, 'expert', [(i, i ^ 1 << apart) for i in range(size)])]
    all_to_all x3, waiting for transfers between devices: 69.5 us -> 120 us  [exchange(): lax.all_to_all(rows.reshape(experts, capacity, features), 'expert', split...]
    pallas_call x0 -> x8, Pallas kernels: none -> 40.4 us  [the longest x3 20.7 us: update(): pl.pallas_call(update_body, grid=(3, rows // tile), in_specs=[pl.BlockSpe...]
    dot_general x5 -> x18, matrix products: 48.8 us -> 86.6 us  [the longest x3 18.5 us: per_device(): part = jnp.einsum('rk,dk->rd', d_both, gate_up, preferred_element_type=F32)]
    unnamed x20 -> x38, local copies, waits for them, and re-layouts: 36.6 us -> 2.04 us
    reduce_scatter x1 -> x3, waiting for transfers between devices: 0.01 us -> 31.3 us  [per_device(): lax.psum_scatter(jnp.concatenate([left.astype(BF), right.astype(BF)], axi...]
    convert_element_type x4 -> x0, other arithmetic: 16.1 us -> none  [the longest x1 4.14 us: per_device(): moment2.astype(jnp.bfloat16)]
  transfers between devices with their start and end apart: 8 -> 14, of which waited for: 6 -> 9; matrix products, arithmetic and copies ran while one was open for 13% -> 23% of each run, Pallas kernels for 0% -> 7%
where the time goes in v1:
time: 433 us; the launch traced here: 427 us
  waiting for transfers between devices  247 us (57%)
  matrix products  86.6 us (20%)
  Pallas kernels  40.4 us (9%)
  starting transfers between devices  24.1 us (6%)
  between operations  15.3 us (4%)
  other arithmetic  10.1 us (2%)
    all_to_all x3, waiting for transfers between devices, exchange(): lax.all_to_all(rows.reshape(experts, capacity, features), 'expert', split...  120 us
    ppermute x5, waiting for transfers between devices, swapped(): lax.ppermute(value, 'expert', [(i, i ^ 1 << apart) for i in range(size)])  79.9 us
    reduce_scatter x3, waiting for transfers between devices, per_device(): lax.psum_scatter(jnp.concatenate([left.astype(BF), right.astype(BF)], axi...  31.3 us
    pallas_call x3, Pallas kernels, update(): pl.pallas_call(update_body, grid=(3, rows // tile), in_specs=[pl.BlockSpe...  20.7 us
    dot_general x3, matrix products, per_device(): part = jnp.einsum('rk,dk->rd', d_both, gate_up, preferred_element_type=F32)  18.5 us
    all_gather x3, waiting for transfers between devices, gathered(): return lax.all_gather(placed, 'dp', axis=0, tiled=True)  15.9 us
    dot_general x3, matrix products, per_device(): pre = jnp.dot(rows_x, gate_up, preferred_element_type=F32)  15.8 us
    all_to_all x3, starting transfers between devices, exchange(): lax.all_to_all(rows.reshape(experts, capacity, features), 'expert', split...  13.9 us
  transfers between devices with their start and end apart: 14, of which 9 were waited for; matrix products, arithmetic and copies ran while one was open for 23% of the time, Pallas kernels for 7%

profile of v1, /device:TPU:0, one launch (start us, length us, event | category | flops | bytes accessed | tf_op | source)
XLA Modules:
  0.0 426.5 jit_solution(16255100547345853586)
XLA Ops:
  15.1 16.5 %collective-permute-done.other_master = bf16[512,768]{1,0:T(8,128)(2,1)S(1)} collective-permute-done((bf16[512,768]{1,0:T(8,128)(2,1)}, bf16[512,768]{1,0:T(8,128)(2,1)S(1)}, u32[]{:S(2)}, u32[]{:S(2)}) %collective-permute-start) | collective-permute-done | bytes 786464 | tf_op jit(solution)/shard_map/ppermute | solution.py:17
  39.5 4.3 %convolution_convert_fusion = bf16[1024,2048]{1,0:T(8,128)(2,1)} fusion(bf16[1,512,2048]{2,1,0:T(8,128)(2,1)S(1)} %copy-done, s32[512]{0:T(512)S(1)} %multiply_add_fusion), kind=kOutput, calls=%fused_computation.1 | convolution fusion | flops 2150105088 | bytes 6293504 | tf_op jit(solution)/shard_map/dot_general | solution.py:130
  43.8 4.7 %all-to-all-start = ((bf16[8,128,2048]{2,1,0:T(8,128)(2,1)}), bf16[8,128,2048]{2,1,0:T(8,128)(2,1)}, u32[]{:S(2)}, u32[]{:S(2)}) async-start(bf16[8,128,2048]{2,1,0:T(8,128)(2,1)} %bitcast.68), calls=%async_computation | async-start | bytes 8388608 | tf_op jit(solution)/shard_map/all_to_all | solution.py:126
  48.6 9.7 %collective-permute-done.1.other_master = bf16[512,768]{1,0:T(8,128)(2,1)S(1)} collective-permute-done((bf16[512,768]{1,0:T(8,128)(2,1)}, bf16[512,768]{1,0:T(8,128)(2,1)S(1)}, u32[]{:S(2)}, u32[]{:S(2)}) %collective-permute-start.1) | collective-permute-done | bytes 786464 | tf_op jit(solution)/shard_map/ppermute | solution.py:17
  63.0 40.0 %all-to-all-done = bf16[8,128,2048]{2,1,0:T(8,128)(2,1)} async-done(((bf16[8,128,2048]{2,1,0:T(8,128)(2,1)}), bf16[8,128,2048]{2,1,0:T(8,128)(2,1)}, u32[]{:S(2)}, u32[]{:S(2)}) %all-to-all-start) | async-done | bytes 4194336 | tf_op jit(solution)/shard_map/all_to_all | solution.py:126
  104.5 4.3 %convolution_convert_fusion.1 = bf16[1024,2048]{1,0:T(8,128)(2,1)} fusion(bf16[1,512,2048]{2,1,0:T(8,128)(2,1)S(1)} %copy-done.11, s32[512]{0:T(512)S(1)} %multiply_add_fusion), kind=kOutput, calls=%fused_computation.2 | convolution fusion | flops 2150105088 | bytes 6293504 | tf_op jit(solution)/shard_map/dot_general | solution.py:131
  108.8 4.7 %all-to-all-start.1 = ((bf16[8,128,2048]{2,1,0:T(8,128)(2,1)}), bf16[8,128,2048]{2,1,0:T(8,128)(2,1)}, u32[]{:S(2)}, u32[]{:S(2)}) async-start(bf16[8,128,2048]{2,1,0:T(8,128)(2,1)} %bitcast.67), calls=%async_computation.1 | async-start | bytes 8388608 | tf_op jit(solution)/shard_map/all_to_all | solution.py:126
  113.6 10.1 %collective-permute-done.2.other_master = bf16[512,768]{1,0:T(8,128)(2,1)S(1)} collective-permute-done((bf16[512,768]{1,0:T(8,128)(2,1)}, bf16[512,768]{1,0:T(8,128)(2,1)S(1)}, u32[]{:S(2)}, u32[]{:S(2)}) %collective-permute-start.2) | collective-permute-done | bytes 786464 | tf_op jit(solution)/shard_map/ppermute | solution.py:17
  125.4 5.3 %fusion.15 = f32[1024,512]{0,1:T(8,128)S(1)} fusion(bf16[1024,2048]{1,0:T(8,128)(2,1)} %bitcast.8, bf16[2048,768]{1,0:T(8,128)(2,1)} %all-gather.4.cloned.1.call-done), kind=kOutput, calls=%fused_computation.28 | convolution fusion | flops 2147483648 | bytes 8388608 | tf_op jit(solution)/shard_map/dot_general | solution.py:157
  130.6 37.0 %all-to-all-done.1 = bf16[8,128,2048]{2,1,0:T(8,128)(2,1)} async-done(((bf16[8,128,2048]{2,1,0:T(8,128)(2,1)}), bf16[8,128,2048]{2,1,0:T(8,128)(2,1)}, u32[]{:S(2)}, u32[]{:S(2)}) %all-to-all-start.1) | async-done | bytes 4194336 | tf_op jit(solution)/shard_map/all_to_all | solution.py:126
  171.6 4.1 multiply_convert_fusion.8
  176.6 4.6 %convolution_convert_fusion.2 = bf16[2048,512]{1,0:T(8,128)(2,1)S(1)} fusion(bf16[1024,2048]{1,0:T(8,128)(2,1)} %bitcast.8, bf16[1024,256]{0,1:T(8,128)(2,1)S(1)} %get-tuple-element.39, bf16[1024,256]{0,1:T(8,128)(2,1)S(1)} %get-tuple-element.38), kind=kOutput, calls=%fused_computation.6 | convolution fusion | flops 2150629376 | bytes 7340032 | tf_op jit(solution)/shard_map/rd,rk->dk/dot_general | solution.py:167
  183.4 5.3 %fusion.11 = f32[1024,512]{0,1:T(8,128)S(1)} fusion(bf16[1024,2048]{1,0:T(8,128)(2,1)} %bitcast.8, bf16[2048,768]{1,0:T(8,128)(2,1)} %all-gather.6.cloned.1.call-done), kind=kOutput, calls=%fused_computation.24 | convolution fusion | flops 2147483648 | bytes 8388608 | tf_op jit(solution)/shard_map/dot_general | solution.py:157
  192.5 4.2 multiply_convert_fusion.6
  197.7 4.6 %convolution_convert_fusion.3 = bf16[2048,512]{1,0:T(8,128)(2,1)S(1)} fusion(bf16[1024,2048]{1,0:T(8,128)(2,1)} %bitcast.8, bf16[1024,256]{0,1:T(8,128)(2,1)S(1)} %get-tuple-element.37, bf16[1024,256]{0,1:T(8,128)(2,1)S(1)} %get-tuple-element.36), kind=kOutput, calls=%fused_computation.7 | convolution fusion | flops 2150629376 | bytes 7340032 | tf_op jit(solution)/shard_map/rd,rk->dk/dot_general | solution.py:167
  204.2 4.6 %shard_map.105 = bf16[512,2304]{1,0:T(8,128)(2,1)} custom-call(f32[512,2304]{1,0:T(8,128)} %bitcast.55), custom_call_target="tpu_custom_call" | custom-call | bytes 7077888 | tf_op jit(solution)/shard_map/pallas_call | solution.py:51
  210.0 15.9 %all-gather.8.cloned.1.call-done = bf16[2048,768]{1,0:T(8,128)(2,1)} async-done(((bf16[512,768]{1,0:T(8,128)(2,1)}), bf16[2048,768]{1,0:T(8,128)(2,1)}) %all-gather.8.cloned.1.call-update) | async-done | bytes 3145744 | tf_op jit(solution)/shard_map/all_gather | solution.py:135
  225.9 5.2 %fusion.5 = f32[1024,512]{0,1:T(8,128)S(1)} fusion(bf16[1024,2048]{1,0:T(8,128)(2,1)} %bitcast.8, bf16[2048,768]{1,0:T(8,128)(2,1)} %all-gather.8.cloned.1.call-done), kind=kOutput, calls=%fused_computation.20 | convolution fusion | flops 2147483648 | bytes 8388608 | tf_op jit(solution)/shard_map/dot_general | solution.py:157
  234.9 4.1 multiply_convert_fusion.4
  239.0 4.6 %convolution_convert_fusion.4 = bf16[2048,512]{1,0:T(8,128)(2,1)S(1)} fusion(bf16[1024,2048]{1,0:T(8,128)(2,1)} %bitcast.8, bf16[1024,256]{0,1:T(8,128)(2,1)S(1)} %get-tuple-element.35, bf16[1024,256]{0,1:T(8,128)(2,1)S(1)} %get-tuple-element.34), kind=kOutput, calls=%fused_computation.8 | convolution fusion | flops 2150629376 | bytes 7340032 | tf_op jit(solution)/shard_map/rd,rk->dk/dot_general | solution.py:167
  245.6 4.5 %fusion.13 = f32[1024,2048]{1,0:T(8,128)S(1)} fusion(bf16[2048,768]{1,0:T(8,128)(2,1)} %all-gather.4.cloned.1.call-done, bf16[1024,256]{0,1:T(8,128)(2,1)} %copy-done.14, bf16[1024,256]{0,1:T(8,128)(2,1)} %copy-done.13), kind=kOutput, calls=%fused_computation.26 | convolution fusion | flops 2149580800 | bytes 11534336 | tf_op jit(solution)/shard_map/rk,dk->rd/dot_general | solution.py:177
  250.1 6.0 %fusion.9 = f32[1024,2048]{1,0:T(8,128)} fusion(bf16[2048,768]{1,0:T(8,128)(2,1)S(1)} %copy-done.10, bf16[1024,256]{0,1:T(8,128)(2,1)S(1)} %copy-done.18, bf16[1024,256]{0,1:T(8,128)(2,1)S(1)} %copy-done.16), kind=kOutput, calls=%fused_computation.22 | convolution fusion | flops 2149580800 | bytes 11534336 | tf_op jit(solution)/shard_map/rk,dk->rd/dot_general | solution.py:177
  256.0 8.1 %add_convert_fusion = bf16[1024,2048]{1,0:T(8,128)(2,1)} fusion(f32[1024,2048]{1,0:T(8,128)S(1)} %fusion.13, f32[1024,2048]{1,0:T(8,128)} %fusion.9, bf16[2048,768]{1,0:T(8,128)(2,1)S(1)} %copy-done.8, bf16[1024,256]{0,1:T(8,128)(2,1)S(1)} %get-tuple-element.35, bf16[1024,256]{0,1:T(8,128)(2,1)S(1)} %get-tuple-element.34), kind=kOutput, calls=%fused_computation | convolution fusion | flops 2155872256 | bytes 24117248 | tf_op jit(solution)/shard_map/rk,dk->rd/dot_general | solution.py:177
  264.2 4.5 %all-to-all-start.2 = ((bf16[8,128,2048]{2,1,0:T(8,128)(2,1)}), bf16[8,128,2048]{2,1,0:T(8,128)(2,1)}, u32[]{:S(2)}, u32[]{:S(2)}) async-start(bf16[8,128,2048]{2,1,0:T(8,128)(2,1)} %bitcast.66), calls=%async_computation.2 | async-start | bytes 8388608 | tf_op jit(solution)/shard_map/all_to_all | solution.py:126
  268.7 4.4 %shard_map.106 = bf16[512,2304]{1,0:T(8,128)(2,1)} custom-call(f32[512,2304]{1,0:T(8,128)} %bitcast.59), custom_call_target="tpu_custom_call" | custom-call | bytes 7077888 | tf_op jit(solution)/shard_map/pallas_call | solution.py:51
  275.0 42.9 %all-to-all-done.2 = bf16[8,128,2048]{2,1,0:T(8,128)(2,1)} async-done(((bf16[8,128,2048]{2,1,0:T(8,128)(2,1)}), bf16[8,128,2048]{2,1,0:T(8,128)(2,1)}, u32[]{:S(2)}, u32[]{:S(2)}) %all-to-all-start.2) | async-done | bytes 4194336 | tf_op jit(solution)/shard_map/all_to_all | solution.py:126
  318.0 5.9 %fusion = bf16[1,512,2048]{2,1,0:T(8,128)(2,1)} fusion(bf16[1024,2048]{1,0:T(8,128)(2,1)} %bitcast.13, s32[512]{0:T(512)S(1)} %multiply_add_fusion), kind=kOutput, calls=%fused_computation.10 | convolution fusion | flops 2149056512 | bytes 6293504 | tf_op jit(solution)/shard_map/dot_general | solution.py:180
  323.8 43.6 %collective-permute-done.4.other_second = bf16[512,2304]{1,0:T(8,128)(2,1)} collective-permute-done((bf16[512,2304]{1,0:T(8,128)(2,1)}, bf16[512,2304]{1,0:T(8,128)(2,1)}, u32[]{:S(2)}, u32[]{:S(2)}) %collective-permute-start.4) | collective-permute-done | bytes 2359328 | tf_op jit(solution)/shard_map/ppermute | solution.py:17
  367.4 6.9 %shard_map.107 = (f32[512,2304]{1,0:T(8,128)}, f32[512,2304]{1,0:T(8,128)}, f32[512,2304]{1,0:T(8,128)}) custom-call(s32[1]{0:T(128)} %bitcast.15.keep, f32[512,2304]{1,0:T(8,128)} %bitcast.52, f32[512,2304]{1,0:T(8,128)} %bitcast.56, f32[512,2304]{1,0:T(8,128)} %bitcast.60, bf16[512,768]{1,0:T(8,128)(2,1)} %copy-done.3, bf16[512,2304]{1,0:T(8,128)(2,1)} %copy-done.2, ...), custom_call_target="tpu_custom_call" | custom-call | flops 7864320 | bytes 12582912 | tf_op jit(solution)/shard_map/pallas_call | solution.py:83
  374.4 6.8 %shard_map.108 = (f32[512,2304]{1,0:T(8,128)}, f32[512,2304]{1,0:T(8,128)}, f32[512,2304]{1,0:T(8,128)}) custom-call(s32[1]{0:T(128)} %bitcast.15.keep, f32[512,2304]{1,0:T(8,128)} %bitcast.53, f32[512,2304]{1,0:T(8,128)} %bitcast.57, f32[512,2304]{1,0:T(8,128)} %bitcast.61, ...), custom_call_target="tpu_custom_call", output_to_operand_aliasing={{0}: (8, {}), {1}: (9, {}), {2}: (10, {})} | custom-call | flops 7864320 | bytes 12582912 | tf_op jit(solution)/shard_map/pallas_call | solution.py:83
  381.2 31.2 %reduce-scatter.4.cloned.1.call-done.grad = bf16[512,768]{1,0:T(8,128)(2,1)} async-done(((bf16[2048,768]{1,0:T(8,128)(2,1)}), bf16[512,768]{1,0:T(8,128)(2,1)}) %reduce-scatter.4.cloned.1.call-update) | async-done | bytes 786448 | tf_op jit(solution)/shard_map/reduce_scatter | solution.py:170
  412.5 6.9 %shard_map.109 = (f32[512,2304]{1,0:T(8,128)}, f32[512,2304]{1,0:T(8,128)}, f32[512,2304]{1,0:T(8,128)}) custom-call(s32[1]{0:T(128)} %bitcast.15.keep, f32[512,2304]{1,0:T(8,128)} %bitcast.54, f32[512,2304]{1,0:T(8,128)} %bitcast.58, f32[512,2304]{1,0:T(8,128)} %bitcast.62, ...), custom_call_target="tpu_custom_call", output_to_operand_aliasing={{0}: (8, {}), {1}: (9, {}), {2}: (10, {})} | custom-call | flops 7864320 | bytes 12582912 | tf_op jit(solution)/shard_map/pallas_call | solution.py:83
  (80 shorter events, 45.6 us)
Async XLA Ops:
  7.2 32.3 %copy-start = (bf16[1,512,2048]{2,1,0:T(8,128)(2,1)S(1)}, bf16[1,512,2048]{2,1,0:T(8,128)(2,1)}, u32[]{:S(2)}) copy-start(bf16[1,512,2048]{2,1,0:T(8,128)(2,1)} %param.7) | copy-start | bytes 6291460
  7.2 118.2 %all-gather.4.cloned.1.call-start = ((), (), s32[]{:S(2)}) async-start(), calls=%async_computation.6 | async-start | bytes 3932160 | tf_op jit(solution)/shard_map/all_gather | solution.py:135
  7.2 6.6 %copy-start.12 = (s32[8]{0:T(128)S(1)}, s32[8]{0:T(128)}, u32[]{:S(2)}) copy-start(s32[8]{0:T(128)} %param.10) | copy-start | bytes 100
  10.9 20.7 %collective-permute-start = (bf16[512,768]{1,0:T(8,128)(2,1)}, bf16[512,768]{1,0:T(8,128)(2,1)S(1)}, u32[]{:S(2)}, u32[]{:S(2)}) collective-permute-start(bf16[512,768]{1,0:T(8,128)(2,1)} %shard_map.102), channel_id=1, source_target_pairs={{0,16},{4,20},{8,24},{12,28},{16,0},{20,4},{24,8},{28,12},{1,17},{... | collective-permute-start | bytes 2359304 | tf_op jit(solution)/shard_map/ppermute | solution.py:17
  31.6 4.6 %copy-start.3 = (bf16[512,768]{1,0:T(8,128)(2,1)}, bf16[512,768]{1,0:T(8,128)(2,1)S(1)}, u32[]{:S(2)}) copy-start(bf16[512,768]{1,0:T(8,128)(2,1)S(1)} %collective-permute-done.other_master) | copy-start | bytes 2359300
  32.6 3.5 copy-start.9
  37.7 20.6 %collective-permute-start.1 = (bf16[512,768]{1,0:T(8,128)(2,1)}, bf16[512,768]{1,0:T(8,128)(2,1)S(1)}, u32[]{:S(2)}, u32[]{:S(2)}) collective-permute-start(bf16[512,768]{1,0:T(8,128)(2,1)} %shard_map.103), channel_id=1, source_target_pairs={{0,16},{4,20},{8,24},{12,28},{16,0},{20,4},{24,8},{28,12},{1,17},{... | collective-permute-start | bytes 2359304 | tf_op jit(solution)/shard_map/ppermute | solution.py:17
  43.8 14.4 %copy-start.4 = (bf16[512,768]{1,0:T(8,128)(2,1)S(1)}, bf16[512,768]{1,0:T(8,128)(2,1)}, u32[]{:S(2)}) copy-start(bf16[512,768]{1,0:T(8,128)(2,1)} %shard_map.103) | copy-start | bytes 2359300
  43.8 59.2 %all-to-all-start = ((bf16[8,128,2048]{2,1,0:T(8,128)(2,1)}), bf16[8,128,2048]{2,1,0:T(8,128)(2,1)}, u32[]{:S(2)}, u32[]{:S(2)}) async-start(bf16[8,128,2048]{2,1,0:T(8,128)(2,1)} %bitcast.68), calls=%async_computation | async-start | bytes 8388608 | tf_op jit(solution)/shard_map/all_to_all | solution.py:126
  48.5 134.9 %all-gather.6.cloned.1.call-start = ((), (), s32[]{:S(2)}) async-start(), calls=%async_computation.7 | async-start | bytes 3932160 | tf_op jit(solution)/shard_map/all_gather | solution.py:135
  58.3 4.8 %copy-start.6 = (bf16[512,768]{1,0:T(8,128)(2,1)}, bf16[512,768]{1,0:T(8,128)(2,1)S(1)}, u32[]{:S(2)}) copy-start(bf16[512,768]{1,0:T(8,128)(2,1)S(1)} %collective-permute-done.1.other_master) | copy-start | bytes 2359300
  59.4 45.1 %copy-start.11 = (bf16[1,512,2048]{2,1,0:T(8,128)(2,1)S(1)}, bf16[1,512,2048]{2,1,0:T(8,128)(2,1)}, u32[]{:S(2)}) copy-start(bf16[1,512,2048]{2,1,0:T(8,128)(2,1)} %param.8) | copy-start | bytes 6291460
  103.0 20.6 %collective-permute-start.2 = (bf16[512,768]{1,0:T(8,128)(2,1)}, bf16[512,768]{1,0:T(8,128)(2,1)S(1)}, u32[]{:S(2)}, u32[]{:S(2)}) collective-permute-start(bf16[512,768]{1,0:T(8,128)(2,1)} %shard_map.104), channel_id=1, source_target_pairs={{0,16},{4,20},{8,24},{12,28},{16,0},{20,4},{24,8},{28,12},{1,17},{... | collective-permute-start | bytes 2359304 | tf_op jit(solution)/shard_map/ppermute | solution.py:17
  108.8 14.9 %copy-start.5 = (bf16[512,768]{1,0:T(8,128)(2,1)S(1)}, bf16[512,768]{1,0:T(8,128)(2,1)}, u32[]{:S(2)}) copy-start(bf16[512,768]{1,0:T(8,128)(2,1)} %shard_map.104) | copy-start | bytes 2359300
  108.8 58.8 %all-to-all-start.1 = ((bf16[8,128,2048]{2,1,0:T(8,128)(2,1)}), bf16[8,128,2048]{2,1,0:T(8,128)(2,1)}, u32[]{:S(2)}, u32[]{:S(2)}) async-start(bf16[8,128,2048]{2,1,0:T(8,128)(2,1)} %bitcast.67), calls=%async_computation.1 | async-start | bytes 8388608 | tf_op jit(solution)/shard_map/all_to_all | solution.py:126
  113.5 112.3 %all-gather.8.cloned.1.call-start = ((), (), s32[]{:S(2)}) async-start(), calls=%async_computation.8 | async-start | bytes 3932160 | tf_op jit(solution)/shard_map/all_gather | solution.py:135
  123.7 7.0 %copy-start.7 = (bf16[512,768]{1,0:T(8,128)(2,1)}, bf16[512,768]{1,0:T(8,128)(2,1)S(1)}, u32[]{:S(2)}) copy-start(bf16[512,768]{1,0:T(8,128)(2,1)S(1)} %collective-permute-done.2.other_master) | copy-start | bytes 2359300
  124.8 242.7 %reduce-scatter.8.cloned.1.call-start = ((), (), s32[]{:S(2)}) async-start(), calls=%async_computation.11 | async-start | bytes 3932160 | tf_op jit(solution)/shard_map/reduce_scatter | solution.py:170
  175.7 1.0 copy-start.14
  183.2 191.2 %reduce-scatter.6.cloned.1.call-start = ((), (), s32[]{:S(2)}) async-start(), calls=%async_computation.10 | async-start | bytes 3932160 | tf_op jit(solution)/shard_map/reduce_scatter | solution.py:170
  196.6 0.8 copy-start.15
  196.6 1.0 copy-start.17
  204.2 208.3 %reduce-scatter.4.cloned.1.call-start = ((), (), s32[]{:S(2)}) async-start(), calls=%async_computation.9 | async-start | bytes 3932160 | tf_op jit(solution)/shard_map/reduce_scatter | solution.py:170
  208.8 64.3 %collective-permute-start.3 = (bf16[512,2304]{1,0:T(8,128)(2,1)}, bf16[512,2304]{1,0:T(8,128)(2,1)S(1)}, u32[]{:S(2)}, u32[]{:S(2)}) collective-permute-start(bf16[512,2304]{1,0:T(8,128)(2,1)} %shard_map.105), channel_id=1, source_target_pairs={{0,16},{4,20},{8,24},{12,28},{16,0},{20,4},{24,8},{28,12},{1,17},{... | collective-permute-start | bytes 7077896 | tf_op jit(solution)/shard_map/ppermute | solution.py:17
  245.5 4.5 %copy-start.10 = (bf16[2048,768]{1,0:T(8,128)(2,1)S(1)}, bf16[2048,768]{1,0:T(8,128)(2,1)}, u32[]{:S(2)}) copy-start(bf16[2048,768]{1,0:T(8,128)(2,1)} %all-gather.6.cloned.1.call-done) | copy-start | bytes 9437188
  245.6 4.5 %copy-start.16 = (bf16[1024,256]{0,1:T(8,128)(2,1)S(1)}, bf16[1024,256]{0,1:T(8,128)(2,1)}, u32[]{:S(2)}) copy-start(bf16[1024,256]{0,1:T(8,128)(2,1)} %copy-done.15) | copy-start | bytes 1572868
  245.6 4.5 %copy-start.18 = (bf16[1024,256]{0,1:T(8,128)(2,1)S(1)}, bf16[1024,256]{0,1:T(8,128)(2,1)}, u32[]{:S(2)}) copy-start(bf16[1024,256]{0,1:T(8,128)(2,1)} %copy-done.17) | copy-start | bytes 1572868
  250.1 6.0 %copy-start.8 = (bf16[2048,768]{1,0:T(8,128)(2,1)S(1)}, bf16[2048,768]{1,0:T(8,128)(2,1)}, u32[]{:S(2)}) copy-start(bf16[2048,768]{1,0:T(8,128)(2,1)} %all-gather.8.cloned.1.call-done) | copy-start | bytes 9437188
  264.2 53.8 %all-to-all-start.2 = ((bf16[8,128,2048]{2,1,0:T(8,128)(2,1)}), bf16[8,128,2048]{2,1,0:T(8,128)(2,1)}, u32[]{:S(2)}, u32[]{:S(2)}) async-start(bf16[8,128,2048]{2,1,0:T(8,128)(2,1)} %bitcast.66), calls=%async_computation.2 | async-start | bytes 8388608 | tf_op jit(solution)/shard_map/all_to_all | solution.py:126
  273.1 50.7 %copy-start.2 = (bf16[512,2304]{1,0:T(8,128)(2,1)}, bf16[512,2304]{1,0:T(8,128)(2,1)S(1)}, u32[]{:S(2)}) copy-start(bf16[512,2304]{1,0:T(8,128)(2,1)S(1)} %collective-permute-done.3.other_first) | copy-start | bytes 7077892
  273.1 94.3 %collective-permute-start.4 = (bf16[512,2304]{1,0:T(8,128)(2,1)}, bf16[512,2304]{1,0:T(8,128)(2,1)}, u32[]{:S(2)}, u32[]{:S(2)}) collective-permute-start(bf16[512,2304]{1,0:T(8,128)(2,1)} %shard_map.106), channel_id=1, source_target_pairs={{0,16},{4,20},{8,24},{12,28},{16,0},{20,4},{24,8},{28,12},{1,17},{... | collective-permute-start | bytes 7077896 | tf_op jit(solution)/shard_map/ppermute | solution.py:17
  412.5 6.9 %copy-start.1 = (bf16[1,512,2048]{2,1,0:T(8,128)(2,1)S(1)}, bf16[1,512,2048]{2,1,0:T(8,128)(2,1)}, u32[]{:S(2)}) copy-start(bf16[1,512,2048]{2,1,0:T(8,128)(2,1)} %param.7) | copy-start | bytes 6291460
  (1 other events, 0.8 us)
Sparse Core Ops, SparseCore 0:
  32.8 64.9 all-gather.3
  99.9 62.1 all-gather.5
  163.7 62.1 all-gather.7
  228.6 58.8 reduce-scatter.7
  289.7 60.2 reduce-scatter.5
  352.2 60.2 reduce-scatter.3

commit v2 on v1

--- a/solution.py
+++ b/solution.py
@@ -96,6 +96,26 @@
     )(keep, *states, *others, grad, *(before or ()))
 
 
+def line_sum(partial):
+    size = lax.axis_size("dp")
+    place = lax.axis_index("dp")
+    rows = partial.shape[0] // size
+
+    def block(owner):
+        return lax.dynamic_slice_in_dim(partial, jnp.clip(owner, 0, size - 1) * rows, rows, 0).astype(F32)
+
+    up = down = jnp.zeros((), F32)
+    for step in range(size - 1):
+        lag = size - 1 - step
+        up_sent = (block(place + lag) + up).astype(BF)
+        down_sent = (block(place - lag) + down).astype(BF)
+        up = lax.ppermute(up_sent, "dp", [(i, i + 1) for i in range(step + 1)]).astype(F32)
+        down = lax.ppermute(
+            down_sent, "dp", [(size - 1 - i, size - 2 - i) for i in range(step + 1)]
+        ).astype(F32)
+    return block(place) + up + down
+
+
 def after(value, *earlier):
     return lax.optimization_barrier((value, *earlier))[0]
 
@@ -141,17 +161,19 @@
     rows_x = exchange(after(send_x, other[0]))
     other[1] = swapped(after(packed[1], other[0]), bit)
     weights[1] = gathered(1, other[1])
-    rows_dy = exchange(after(send_dy, rows_x))
+    narrow_first = narrow(states[1])
+    narrow_second = narrow(states[2])
+    rows_dy = exchange(after(send_dy, rows_x, narrow_first, narrow_second))
     other[2] = swapped(after(packed[2], rows_x), bit)
     weights[2] = gathered(2, other[2])
-    narrow_first = narrow(states[1])
-    narrow_second = narrow(states[2])
     other_first = swapped(after(narrow_first, rows_dy), bit)
     other_second = swapped(after(narrow_second, other_first), bit)
 
     total = None
     grads = []
     for c in range(CHUNKS):
+        if c == CHUNKS - 1:
+            rows_x = after(rows_x, other_first)
         gate_up = weights[c][:, : 2 * width]
         down = weights[c][:, 2 * width :]
         pre = jnp.dot(rows_x, gate_up, preferred_element_type=F32)
@@ -166,18 +188,15 @@
         d_both = jnp.concatenate([d_gate, d_up], axis=1)
         left = jnp.einsum("rd,rk->dk", rows_x, d_both, preferred_element_type=F32)
         right = jnp.einsum("rd,rk->dk", rows_dy, hidden, preferred_element_type=F32)
-        grads.append(
-            lax.psum_scatter(
-                jnp.concatenate([left.astype(BF), right.astype(BF)], axis=1),
-                "dp",
-                scatter_dimension=0,
-                tiled=True,
-            )
-        )
+        partial = jnp.concatenate([left.astype(BF), right.astype(BF)], axis=1)
+        if c % 2 == 1:
+            grads.append(lax.psum_scatter(partial, "dp", scatter_dimension=0, tiled=True))
+        else:
+            grads.append(line_sum(partial))
         part = jnp.einsum("rk,dk->rd", d_both, gate_up, preferred_element_type=F32)
         total = part if total is None else total + part
     returned = exchange(total.astype(BF))
-    token_grad = jnp.dot(take, returned, preferred_element_type=F32).astype(BF)
+    token_grad = jnp.dot(take, after(returned, grads[-1]), preferred_element_type=F32).astype(BF)
 
     made = None
     for c in range(CHUNKS):

time: 433 us -> 454 us (1.048)
  waiting for transfers between devices: 247 us -> 209 us
  starting transfers between devices: 24.1 us -> 57.1 us
  other arithmetic: 10.1 us -> 26.1 us
  matrix products: 86.6 us -> 96.2 us
    all_to_all x3, waiting for transfers between devices: 120 us -> 0.01 us  [exchange(): lax.all_to_all(rows.reshape(experts, capacity, features), 'expert', split...]
    ppermute x5, waiting for transfers between devices: 79.9 us -> 161 us  [swapped(): lax.ppermute(value, 'expert', [(i, i ^ 1 << apart) for i in range(size)])]
    ppermute x0 -> x12, waiting for transfers between devices: none -> 47.5 us  [the longest x6 47.5 us: line_sum(): lax.ppermute(up_sent, 'dp', [(i, i + 1) for i in range(step + 1)])]
    ppermute x0 -> x12, starting transfers between devices: none -> 34 us  [the longest x6 24.8 us: line_sum(): lax.ppermute(up_sent, 'dp', [(i, i + 1) for i in range(step + 1)])]
    reduce_scatter x3 -> x1, waiting for transfers between devices: 31.3 us -> 0.01 us  [per_device(): lax.psum_scatter(partial, 'dp', scatter_dimension=0, tiled=True)]
    all_gather x3, waiting for transfers between devices: 15.9 us -> 0.02 us  [gathered(): return lax.all_gather(placed, 'dp', axis=0, tiled=True)]
    convert_element_type x0 -> x4, other arithmetic: none -> 11.7 us  [line_sum(): up_sent = (block(place + lag) + up).astype(BF)]
    add x0 -> x2, other arithmetic: none -> 5.61 us  [line_sum(): return block(place) + up + down]
  transfers between devices with their start and end apart: 14 -> 24, of which waited for: 9 -> 10; matrix products, arithmetic and copies ran while one was open for 23% -> 27% of each run, Pallas kernels for 7% -> 5%
where the time goes in v2:
time: 454 us; the launch traced here: 446 us
  waiting for transfers between devices  209 us (46%)
  matrix products  96.2 us (21%)
  starting transfers between devices  57.1 us (13%)
  Pallas kernels  41 us (9%)
  other arithmetic  26.1 us (6%)
  between operations  15.1 us (3%)
    ppermute x5, waiting for transfers between devices, swapped(): lax.ppermute(value, 'expert', [(i, i ^ 1 << apart) for i in range(size)])  161 us
    ppermute x6, waiting for transfers between devices, line_sum(): lax.ppermute(up_sent, 'dp', [(i, i + 1) for i in range(step + 1)])  47.5 us
    ppermute x6, starting transfers between devices, line_sum(): lax.ppermute(up_sent, 'dp', [(i, i + 1) for i in range(step + 1)])  24.8 us
    dot_general x3, matrix products, per_device(): part = jnp.einsum('rk,dk->rd', d_both, gate_up, preferred_element_type=F32)  22 us
    pallas_call x3, Pallas kernels, update(): pl.pallas_call(update_body, grid=(3, rows // tile), in_specs=[pl.BlockSpe...  21.4 us
    dot_general x3, matrix products, per_device(): pre = jnp.dot(rows_x, gate_up, preferred_element_type=F32)  19.6 us
    dot_general x3, matrix products, per_device(): left = jnp.einsum('rd,rk->dk', rows_x, d_both, preferred_element_type=F32)  14.7 us
    all_to_all x3, starting transfers between devices, exchange(): lax.all_to_all(rows.reshape(experts, capacity, features), 'expert', split...  13.8 us
  transfers between devices with their start and end apart: 24, of which 10 were waited for; matrix products, arithmetic and copies ran while one was open for 27% of the time, Pallas kernels for 5%

profile of v2, /device:TPU:0, one launch (start us, length us, event | category | flops | bytes accessed | tf_op | source)
XLA Modules:
  0.0 446.1 jit_solution(4162041670053339483)
XLA Ops:
  15.1 16.5 %collective-permute-done.other_master = bf16[512,768]{1,0:T(8,128)(2,1)S(1)} collective-permute-done((bf16[512,768]{1,0:T(8,128)(2,1)}, bf16[512,768]{1,0:T(8,128)(2,1)S(1)}, u32[]{:S(2)}, u32[]{:S(2)}) %collective-permute-start) | collective-permute-done | bytes 786464 | tf_op jit(solution)/shard_map/ppermute | solution.py:17
  38.5 4.6 %all-to-all-start = ((bf16[8,128,2048]{2,1,0:T(8,128)(2,1)}), bf16[8,128,2048]{2,1,0:T(8,128)(2,1)}, u32[]{:S(2)}, u32[]{:S(2)}) async-start(bf16[8,128,2048]{2,1,0:T(8,128)(2,1)} %bitcast.70), calls=%async_computation | async-start | bytes 8388608 | tf_op jit(solution)/shard_map/all_to_all | solution.py:146
  48.6 59.5 %collective-permute-done.1.other_master = bf16[512,768]{1,0:T(8,128)(2,1)S(1)} collective-permute-done((bf16[512,768]{1,0:T(8,128)(2,1)}, bf16[512,768]{1,0:T(8,128)(2,1)S(1)}, u32[]{:S(2)}, u32[]{:S(2)}) %collective-permute-start.1) | collective-permute-done | bytes 786464 | tf_op jit(solution)/shard_map/ppermute | solution.py:17
  114.4 4.6 %shard_map.104 = bf16[512,2304]{1,0:T(8,128)(2,1)} custom-call(f32[512,2304]{1,0:T(8,128)} %bitcast.59), custom_call_target="tpu_custom_call" | custom-call | bytes 7077888 | tf_op jit(solution)/shard_map/pallas_call | solution.py:51
  123.3 4.6 %all-to-all-start.1 = ((bf16[8,128,2048]{2,1,0:T(8,128)(2,1)}), bf16[8,128,2048]{2,1,0:T(8,128)(2,1)}, u32[]{:S(2)}, u32[]{:S(2)}) async-start(bf16[8,128,2048]{2,1,0:T(8,128)(2,1)} %bitcast.69), calls=%async_computation.1 | async-start | bytes 8388608 | tf_op jit(solution)/shard_map/all_to_all | solution.py:146
  133.3 59.5 %collective-permute-done.2.other_master = bf16[512,768]{1,0:T(8,128)(2,1)S(1)} collective-permute-done((bf16[512,768]{1,0:T(8,128)(2,1)}, bf16[512,768]{1,0:T(8,128)(2,1)S(1)}, u32[]{:S(2)}, u32[]{:S(2)}) %collective-permute-start.2) | collective-permute-done | bytes 786464 | tf_op jit(solution)/shard_map/ppermute | solution.py:17
  194.2 6.6 %fusion.15 = f32[1024,512]{0,1:T(8,128)} fusion(bf16[1024,2048]{1,0:T(8,128)(2,1)} %bitcast.8, bf16[2048,768]{1,0:T(8,128)(2,1)} %all-gather.4.cloned.1.call-done), kind=kOutput, calls=%fused_computation.54 | convolution fusion | flops 2147483648 | bytes 8388608 | tf_op jit(solution)/shard_map/dot_general | solution.py:179
  200.8 7.1 %fusion.11 = f32[1024,512]{0,1:T(8,128)} fusion(bf16[1024,2048]{1,0:T(8,128)(2,1)} %bitcast.8, bf16[2048,768]{1,0:T(8,128)(2,1)} %all-gather.6.cloned.1.call-done), kind=kOutput, calls=%fused_computation.50 | convolution fusion | flops 2147483648 | bytes 8388608 | tf_op jit(solution)/shard_map/dot_general | solution.py:179
  215.8 5.0 %convolution_convert_fusion.2 = bf16[2048,512]{1,0:T(8,128)(2,1)S(1)} fusion(bf16[1024,2048]{1,0:T(8,128)(2,1)} %bitcast.8, bf16[1024,256]{0,1:T(8,128)(2,1)S(1)} %get-tuple-element.55, bf16[1024,256]{0,1:T(8,128)(2,1)S(1)} %get-tuple-element.54), kind=kOutput, calls=%fused_computation.32 | convolution fusion | flops 2150629376 | bytes 7340032 | tf_op jit(solution)/shard_map/rd,rk->dk/dot_general | solution.py:189
  222.1 4.6 %collective-permute-start.11 = (bf16[512,768]{1,0:T(8,128)(2,1)}, bf16[512,768]{1,0:T(8,128)(2,1)}, u32[]{:S(2)}, u32[]{:S(2)}) collective-permute-start(bf16[512,768]{1,0:T(8,128)(2,1)} %get-tuple-element.42), channel_id=1, source_target_pairs={{0,1},{4,5},{8,9},{12,13},{16,17},{20,21},{24,25},{28,29}} | collective-permute-start | bytes 2359304 | tf_op jit(solution)/shard_map/ppermute | solution.py:112
  237.1 4.6 %convolution_convert_fusion.3 = bf16[2048,512]{1,0:T(8,128)(2,1)S(1)} fusion(bf16[1024,2048]{1,0:T(8,128)(2,1)} %bitcast.8, bf16[1024,256]{0,1:T(8,128)(2,1)S(1)} %get-tuple-element.53, bf16[1024,256]{0,1:T(8,128)(2,1)S(1)} %get-tuple-element.52), kind=kOutput, calls=%fused_computation.33 | convolution fusion | flops 2150629376 | bytes 7340032 | tf_op jit(solution)/shard_map/rd,rk->dk/dot_general | solution.py:189
  243.6 7.8 %fusion.9 = f32[1024,2048]{1,0:T(8,128)} fusion(bf16[2048,768]{1,0:T(8,128)(2,1)} %all-gather.6.cloned.1.call-done, bf16[1024,256]{0,1:T(8,128)(2,1)} %copy-done.25, bf16[1024,256]{0,1:T(8,128)(2,1)} %copy-done.24), kind=kOutput, calls=%fused_computation.48 | convolution fusion | flops 2149580800 | bytes 11534336 | tf_op jit(solution)/shard_map/rk,dk->rd/dot_general | solution.py:196
  251.5 5.7 %fusion.13 = f32[1024,2048]{1,0:T(8,128)} fusion(bf16[2048,768]{1,0:T(8,128)(2,1)S(1)} %copy-done.17, bf16[1024,256]{0,1:T(8,128)(2,1)S(1)} %copy-done.23, bf16[1024,256]{0,1:T(8,128)(2,1)S(1)} %copy-done.21), kind=kOutput, calls=%fused_computation.52 | convolution fusion | flops 2149580800 | bytes 11534336 | tf_op jit(solution)/shard_map/rk,dk->rd/dot_general | solution.py:196
  257.2 24.2 %collective-permute-done.3.other_first = bf16[512,2304]{1,0:T(8,128)(2,1)} collective-permute-done((bf16[512,2304]{1,0:T(8,128)(2,1)}, bf16[512,2304]{1,0:T(8,128)(2,1)}, u32[]{:S(2)}, u32[]{:S(2)}) %collective-permute-start.3) | collective-permute-done | bytes 2359328 | tf_op jit(solution)/shard_map/ppermute | solution.py:17
  281.3 5.9 %fusion.5 = f32[1024,512]{0,1:T(8,128)S(1)} fusion(bf16[1024,2048]{1,0:T(8,128)(2,1)} %bitcast.8, bf16[2048,768]{1,0:T(8,128)(2,1)} %all-gather.8.cloned.1.call-done), kind=kOutput, calls=%fused_computation.46 | convolution fusion | flops 2147483648 | bytes 8388608 | tf_op jit(solution)/shard_map/dot_general | solution.py:179
  287.3 4.7 %multiply_convert_fusion.4 = (bf16[1024,256]{0,1:T(8,128)(2,1)S(1)}, bf16[1024,256]{0,1:T(8,128)(2,1)S(1)}) fusion(f32[1024,512]{0,1:T(8,128)S(1)} %fusion.5, bf16[1024,2048]{1,0:T(8,128)(2,1)} %bitcast.12, bf16[2048,768]{1,0:T(8,128)(2,1)S(1)} %copy-done.13), kind=kOutput, calls=%fused_computation.79 | convolution fusion | flops 1077149696 | bytes 8388608 | tf_op jit(solution)/shard_map/dot_general | solution.py:185
  292.1 8.5 %add_convert_fusion = bf16[1024,2048]{1,0:T(8,128)(2,1)} fusion(f32[1024,2048]{1,0:T(8,128)} %fusion.13, f32[1024,2048]{1,0:T(8,128)S(1)} %bitcast.68, bf16[2048,768]{1,0:T(8,128)(2,1)S(1)} %copy-done.13, bf16[1024,256]{0,1:T(8,128)(2,1)S(1)} %get-tuple-element.51, bf16[1024,256]{0,1:T(8,128)(2,1)S(1)} %get-tuple-element.50), kind=kOutput, calls=%fused_computation | convolution fusion | flops 2155872256 | bytes 24117248 | tf_op jit(solution)/shard_map/rk,dk->rd/dot_general | solution.py:196
  300.6 4.6 %all-to-all-start.2 = ((bf16[8,128,2048]{2,1,0:T(8,128)(2,1)}), bf16[8,128,2048]{2,1,0:T(8,128)(2,1)}, u32[]{:S(2)}, u32[]{:S(2)}) async-start(bf16[8,128,2048]{2,1,0:T(8,128)(2,1)} %bitcast.66), calls=%async_computation.2 | async-start | bytes 8388608 | tf_op jit(solution)/shard_map/all_to_all | solution.py:146
  305.2 5.0 %convolution_convert_fusion.5 = bf16[2048,512]{1,0:T(8,128)(2,1)S(1)} fusion(bf16[1024,2048]{1,0:T(8,128)(2,1)} %bitcast.8, bf16[1024,256]{0,1:T(8,128)(2,1)} %copy-done.15, bf16[1024,256]{0,1:T(8,128)(2,1)} %copy-done.14), kind=kOutput, calls=%fused_computation.35 | convolution fusion | flops 2150629376 | bytes 7340032 | tf_op jit(solution)/shard_map/rd,rk->dk/dot_general | solution.py:189
  310.2 4.5 %convolution_convert_fusion.8 = bf16[2048,256]{1,0:T(8,128)(2,1)S(1)} fusion(bf16[1024,2048]{1,0:T(8,128)(2,1)} %bitcast.12, f32[1024,512]{0,1:T(8,128)S(1)} %copy-done.28), kind=kOutput, calls=%fused_computation.39 | convolution fusion | flops 1075838976 | bytes 7340032 | tf_op jit(solution)/shard_map/rd,rk->dk/dot_general | solution.py:190
  328.6 20.6 %collective-permute-done.4 = bf16[512,768]{1,0:T(8,128)(2,1)} collective-permute-done((bf16[512,768]{1,0:T(8,128)(2,1)}, bf16[512,768]{1,0:T(8,128)(2,1)}, u32[]{:S(2)}, u32[]{:S(2)}) %collective-permute-start.4) | collective-permute-done | bytes 786464 | tf_op jit(solution)/shard_map/ppermute | solution.py:112
  352.2 5.3 %collective-permute-start.5 = (bf16[512,768]{1,0:T(8,128)(2,1)}, bf16[512,768]{1,0:T(8,128)(2,1)}, u32[]{:S(2)}, u32[]{:S(2)}) collective-permute-start(bf16[512,768]{1,0:T(8,128)(2,1)} %get-tuple-element.46), channel_id=1, source_target_pairs={{0,1},{1,2},{4,5},{5,6},{8,9},{9,10},{12,13},{13,14},{16,17},{17,1... | collective-permute-start | bytes 2359304 | tf_op jit(solution)/shard_map/ppermute | solution.py:112
  359.1 7.0 %collective-permute-done.12 = bf16[512,768]{1,0:T(8,128)(2,1)} collective-permute-done((bf16[512,768]{1,0:T(8,128)(2,1)}, bf16[512,768]{1,0:T(8,128)(2,1)}, u32[]{:S(2)}, u32[]{:S(2)}) %collective-permute-start.12) | collective-permute-done | bytes 786464 | tf_op jit(solution)/shard_map/ppermute | solution.py:112
  369.0 5.3 %collective-permute-start.13 = (bf16[512,768]{1,0:T(8,128)(2,1)}, bf16[512,768]{1,0:T(8,128)(2,1)}, u32[]{:S(2)}, u32[]{:S(2)}) collective-permute-start(bf16[512,768]{1,0:T(8,128)(2,1)} %get-tuple-element.38), channel_id=1, source_target_pairs={{0,1},{1,2},{2,3},{4,5},{5,6},{6,7},{8,9},{9,10},{10,11},{12,13},{... | collective-permute-start | bytes 2359304 | tf_op jit(solution)/shard_map/ppermute | solution.py:112
  375.6 7.4 %collective-permute-done.5 = bf16[512,768]{1,0:T(8,128)(2,1)} collective-permute-done((bf16[512,768]{1,0:T(8,128)(2,1)}, bf16[512,768]{1,0:T(8,128)(2,1)}, u32[]{:S(2)}, u32[]{:S(2)}) %collective-permute-start.5) | collective-permute-done | bytes 786464 | tf_op jit(solution)/shard_map/ppermute | solution.py:112
  385.9 5.3 %collective-permute-start.6 = (bf16[512,768]{1,0:T(8,128)(2,1)}, bf16[512,768]{1,0:T(8,128)(2,1)}, u32[]{:S(2)}, u32[]{:S(2)}) collective-permute-start(bf16[512,768]{1,0:T(8,128)(2,1)} %get-tuple-element.44), channel_id=1, source_target_pairs={{0,1},{1,2},{2,3},{4,5},{5,6},{6,7},{8,9},{9,10},{10,11},{12,13},{... | collective-permute-start | bytes 2359304 | tf_op jit(solution)/shard_map/ppermute | solution.py:112
  392.7 7.1 %collective-permute-done.13 = bf16[512,768]{1,0:T(8,128)(2,1)} collective-permute-done((bf16[512,768]{1,0:T(8,128)(2,1)}, bf16[512,768]{1,0:T(8,128)(2,1)}, u32[]{:S(2)}, u32[]{:S(2)}) %collective-permute-start.13) | collective-permute-done | bytes 786464 | tf_op jit(solution)/shard_map/ppermute | solution.py:112
  403.9 7.4 %shard_map.107 = (f32[512,2304]{1,0:T(8,128)}, f32[512,2304]{1,0:T(8,128)}, f32[512,2304]{1,0:T(8,128)}) custom-call(s32[1]{0:T(128)} %bitcast.17.keep, f32[512,2304]{1,0:T(8,128)} %bitcast.52, f32[512,2304]{1,0:T(8,128)} %bitcast.56, f32[512,2304]{1,0:T(8,128)} %bitcast.60, bf16[512,768]{1,0:T(8,128)(2,1)} %copy-done.10, ...), custom_call_target="tpu_custom_call" | custom-call | flops 7864320 | bytes 12582912 | tf_op jit(solution)/shard_map/pallas_call | solution.py:83
  411.3 5.4 %collective-permute-done.6 = bf16[512,768]{1,0:T(8,128)(2,1)} collective-permute-done((bf16[512,768]{1,0:T(8,128)(2,1)}, bf16[512,768]{1,0:T(8,128)(2,1)}, u32[]{:S(2)}, u32[]{:S(2)}) %collective-permute-start.6) | collective-permute-done | bytes 786464 | tf_op jit(solution)/shard_map/ppermute | solution.py:112
  419.4 5.9 %fusion = bf16[1,512,2048]{2,1,0:T(8,128)(2,1)} fusion(bf16[1024,2048]{1,0:T(8,128)(2,1)} %bitcast.15, s32[512]{0:T(512)S(1)} %multiply_add_fusion), kind=kOutput, calls=%fused_computation.36 | convolution fusion | flops 2149056512 | bytes 6293504 | tf_op jit(solution)/shard_map/dot_general | solution.py:199
  425.3 6.8 %shard_map.108 = (f32[512,2304]{1,0:T(8,128)}, f32[512,2304]{1,0:T(8,128)}, f32[512,2304]{1,0:T(8,128)}) custom-call(s32[1]{0:T(128)} %bitcast.17.keep, f32[512,2304]{1,0:T(8,128)} %bitcast.53, f32[512,2304]{1,0:T(8,128)} %bitcast.57, f32[512,2304]{1,0:T(8,128)} %bitcast.61, ...), custom_call_target="tpu_custom_call", output_to_operand_aliasing={{0}: (8, {}), {1}: (9, {}), {2}: (10, {})} | custom-call | flops 7864320 | bytes 12582912 | tf_op jit(solution)/shard_map/pallas_call | solution.py:83
  432.1 7.2 %shard_map.109 = (f32[512,2304]{1,0:T(8,128)}, f32[512,2304]{1,0:T(8,128)}, f32[512,2304]{1,0:T(8,128)}) custom-call(s32[1]{0:T(128)} %bitcast.17.keep, f32[512,2304]{1,0:T(8,128)} %bitcast.54, f32[512,2304]{1,0:T(8,128)} %bitcast.58, f32[512,2304]{1,0:T(8,128)} %bitcast.62, ...), custom_call_target="tpu_custom_call", output_to_operand_aliasing={{0}: (8, {}), {1}: (9, {}), {2}: (10, {})} | custom-call | flops 7864320 | bytes 12582912 | tf_op jit(solution)/shard_map/pallas_call | solution.py:83
  (131 shorter events, 92.2 us)
Async XLA Ops:
  7.2 27.0 %copy-start = (bf16[1,512,2048]{2,1,0:T(8,128)(2,1)S(1)}, bf16[1,512,2048]{2,1,0:T(8,128)(2,1)}, u32[]{:S(2)}) copy-start(bf16[1,512,2048]{2,1,0:T(8,128)(2,1)} %param.7) | copy-start | bytes 6291460
  7.2 187.0 %all-gather.4.cloned.1.call-start = ((), (), s32[]{:S(2)}) async-start(), calls=%async_computation.4 | async-start | bytes 3932160 | tf_op jit(solution)/shard_map/all_gather | solution.py:155
  10.9 21.8 %copy-start.16 = (s32[1,512,1]{1,2,0:T(1,128)S(1)}, s32[1,512,1]{1,2,0:T(1,128)}, u32[]{:S(2)}) copy-start(s32[1,512,1]{1,2,0:T(1,128)} %param.9) | copy-start | bytes 6148
  10.9 20.7 %collective-permute-start = (bf16[512,768]{1,0:T(8,128)(2,1)}, bf16[512,768]{1,0:T(8,128)(2,1)S(1)}, u32[]{:S(2)}, u32[]{:S(2)}) collective-permute-start(bf16[512,768]{1,0:T(8,128)(2,1)} %shard_map.102), channel_id=1, source_target_pairs={{0,16},{4,20},{8,24},{12,28},{16,0},{20,4},{24,8},{28,12},{1,17},{... | collective-permute-start | bytes 2359304 | tf_op jit(solution)/shard_map/ppermute | solution.py:17
  38.5 84.8 %all-to-all-start = ((bf16[8,128,2048]{2,1,0:T(8,128)(2,1)}), bf16[8,128,2048]{2,1,0:T(8,128)(2,1)}, u32[]{:S(2)}, u32[]{:S(2)}) async-start(bf16[8,128,2048]{2,1,0:T(8,128)(2,1)} %bitcast.70), calls=%async_computation | async-start | bytes 8388608 | tf_op jit(solution)/shard_map/all_to_all | solution.py:146
  43.1 157.6 %all-gather.6.cloned.1.call-start = ((), (), s32[]{:S(2)}) async-start(), calls=%async_computation.5 | async-start | bytes 3932160 | tf_op jit(solution)/shard_map/all_gather | solution.py:155
  46.7 61.3 %collective-permute-start.1 = (bf16[512,768]{1,0:T(8,128)(2,1)}, bf16[512,768]{1,0:T(8,128)(2,1)S(1)}, u32[]{:S(2)}, u32[]{:S(2)}) collective-permute-start(bf16[512,768]{1,0:T(8,128)(2,1)} %shard_map.105), channel_id=1, source_target_pairs={{0,16},{4,20},{8,24},{12,28},{16,0},{20,4},{24,8},{28,12},{1,17},{... | collective-permute-start | bytes 2359304 | tf_op jit(solution)/shard_map/ppermute | solution.py:17
  123.3 84.6 %all-to-all-start.1 = ((bf16[8,128,2048]{2,1,0:T(8,128)(2,1)}), bf16[8,128,2048]{2,1,0:T(8,128)(2,1)}, u32[]{:S(2)}, u32[]{:S(2)}) async-start(bf16[8,128,2048]{2,1,0:T(8,128)(2,1)} %bitcast.69), calls=%async_computation.1 | async-start | bytes 8388608 | tf_op jit(solution)/shard_map/all_to_all | solution.py:146
  127.9 153.4 %all-gather.8.cloned.1.call-start = ((), (), s32[]{:S(2)}) async-start(), calls=%async_computation.6 | async-start | bytes 3932160 | tf_op jit(solution)/shard_map/all_gather | solution.py:155
  131.5 61.4 %collective-permute-start.2 = (bf16[512,768]{1,0:T(8,128)(2,1)}, bf16[512,768]{1,0:T(8,128)(2,1)S(1)}, u32[]{:S(2)}, u32[]{:S(2)}) collective-permute-start(bf16[512,768]{1,0:T(8,128)(2,1)} %shard_map.106), channel_id=1, source_target_pairs={{0,16},{4,20},{8,24},{12,28},{16,0},{20,4},{24,8},{28,12},{1,17},{... | collective-permute-start | bytes 2359304 | tf_op jit(solution)/shard_map/ppermute | solution.py:17
  194.0 231.4 %reduce-scatter.2.cloned.1.call-start = ((), (), s32[]{:S(2)}) async-start(), calls=%async_computation.7 | async-start | bytes 3932160 | tf_op jit(solution)/shard_map/reduce_scatter | solution.py:193
  222.1 99.8 %collective-permute-start.11 = (bf16[512,768]{1,0:T(8,128)(2,1)}, bf16[512,768]{1,0:T(8,128)(2,1)}, u32[]{:S(2)}, u32[]{:S(2)}) collective-permute-start(bf16[512,768]{1,0:T(8,128)(2,1)} %get-tuple-element.42), channel_id=1, source_target_pairs={{0,1},{4,5},{8,9},{12,13},{16,17},{20,21},{24,25},{28,29}} | collective-permute-start | bytes 2359304 | tf_op jit(solution)/shard_map/ppermute | solution.py:112
  226.6 95.3 %collective-permute-start.14 = (bf16[512,768]{1,0:T(8,128)(2,1)}, bf16[512,768]{1,0:T(8,128)(2,1)}, u32[]{:S(2)}, u32[]{:S(2)}) collective-permute-start(bf16[512,768]{1,0:T(8,128)(2,1)} %get-tuple-element.43), channel_id=1, source_target_pairs={{3,2},{7,6},{11,10},{15,14},{19,18},{23,22},{27,26},{31,30}} | collective-permute-start | bytes 2359304 | tf_op jit(solution)/shard_map/ppermute | solution.py:113
  228.4 52.9 %collective-permute-start.3 = (bf16[512,2304]{1,0:T(8,128)(2,1)}, bf16[512,2304]{1,0:T(8,128)(2,1)}, u32[]{:S(2)}, u32[]{:S(2)}) collective-permute-start(bf16[512,2304]{1,0:T(8,128)(2,1)} %shard_map.103), channel_id=1, source_target_pairs={{0,16},{4,20},{8,24},{12,28},{16,0},{20,4},{24,8},{28,12},{1,17},{... | collective-permute-start | bytes 7077896 | tf_op jit(solution)/shard_map/ppermute | solution.py:17
  300.6 118.9 %all-to-all-start.2 = ((bf16[8,128,2048]{2,1,0:T(8,128)(2,1)}), bf16[8,128,2048]{2,1,0:T(8,128)(2,1)}, u32[]{:S(2)}, u32[]{:S(2)}) async-start(bf16[8,128,2048]{2,1,0:T(8,128)(2,1)} %bitcast.66), calls=%async_computation.2 | async-start | bytes 8388608 | tf_op jit(solution)/shard_map/all_to_all | solution.py:146
  316.3 33.0 %collective-permute-start.4 = (bf16[512,768]{1,0:T(8,128)(2,1)}, bf16[512,768]{1,0:T(8,128)(2,1)}, u32[]{:S(2)}, u32[]{:S(2)}) collective-permute-start(bf16[512,768]{1,0:T(8,128)(2,1)} %get-tuple-element.48), channel_id=1, source_target_pairs={{0,1},{4,5},{8,9},{12,13},{16,17},{20,21},{24,25},{28,29}} | collective-permute-start | bytes 2359304 | tf_op jit(solution)/shard_map/ppermute | solution.py:112
  318.5 30.8 %collective-permute-start.7 = (bf16[512,768]{1,0:T(8,128)(2,1)}, bf16[512,768]{1,0:T(8,128)(2,1)}, u32[]{:S(2)}, u32[]{:S(2)}) collective-permute-start(bf16[512,768]{1,0:T(8,128)(2,1)} %get-tuple-element.49), channel_id=1, source_target_pairs={{3,2},{7,6},{11,10},{15,14},{19,18},{23,22},{27,26},{31,30}} | collective-permute-start | bytes 2359304 | tf_op jit(solution)/shard_map/ppermute | solution.py:113
  320.0 29.2 %copy-start.3 = (bf16[2048,512]{1,0:T(8,128)(2,1)S(1)}, bf16[2048,512]{1,0:T(8,128)(2,1)}, u32[]{:S(2)}) copy-start(bf16[2048,512]{1,0:T(8,128)(2,1)} %copy-done.2) | copy-start | bytes 6291460
  320.0 29.2 %copy-start.7 = (bf16[2048,256]{1,0:T(8,128)(2,1)S(1)}, bf16[2048,256]{1,0:T(8,128)(2,1)}, u32[]{:S(2)}) copy-start(bf16[2048,256]{1,0:T(8,128)(2,1)} %copy-done.6) | copy-start | bytes 3145732
  320.0 83.9 %collective-permute-start.10 = (bf16[512,2304]{1,0:T(8,128)(2,1)}, bf16[512,2304]{1,0:T(8,128)(2,1)}, u32[]{:S(2)}, u32[]{:S(2)}) collective-permute-start(bf16[512,2304]{1,0:T(8,128)(2,1)} %shard_map.104), channel_id=1, source_target_pairs={{0,16},{4,20},{8,24},{12,28},{16,0},{20,4},{24,8},{28,12},{1,17},{... | collective-permute-start | bytes 7077896 | tf_op jit(solution)/shard_map/ppermute | solution.py:17
  324.9 41.2 %collective-permute-start.12 = (bf16[512,768]{1,0:T(8,128)(2,1)}, bf16[512,768]{1,0:T(8,128)(2,1)}, u32[]{:S(2)}, u32[]{:S(2)}) collective-permute-start(bf16[512,768]{1,0:T(8,128)(2,1)} %get-tuple-element.40), channel_id=1, source_target_pairs={{0,1},{1,2},{4,5},{5,6},{8,9},{9,10},{12,13},{13,14},{16,17},{17,1... | collective-permute-start | bytes 2359304 | tf_op jit(solution)/shard_map/ppermute | solution.py:112
  327.1 39.1 %collective-permute-start.15 = (bf16[512,768]{1,0:T(8,128)(2,1)}, bf16[512,768]{1,0:T(8,128)(2,1)}, u32[]{:S(2)}, u32[]{:S(2)}) collective-permute-start(bf16[512,768]{1,0:T(8,128)(2,1)} %get-tuple-element.41), channel_id=1, source_target_pairs={{3,2},{2,1},{7,6},{6,5},{11,10},{10,9},{15,14},{14,13},{19,18},{18... | collective-permute-start | bytes 2359304 | tf_op jit(solution)/shard_map/ppermute | solution.py:113
  352.2 30.8 %collective-permute-start.5 = (bf16[512,768]{1,0:T(8,128)(2,1)}, bf16[512,768]{1,0:T(8,128)(2,1)}, u32[]{:S(2)}, u32[]{:S(2)}) collective-permute-start(bf16[512,768]{1,0:T(8,128)(2,1)} %get-tuple-element.46), channel_id=1, source_target_pairs={{0,1},{1,2},{4,5},{5,6},{8,9},{9,10},{12,13},{13,14},{16,17},{17,1... | collective-permute-start | bytes 2359304 | tf_op jit(solution)/shard_map/ppermute | solution.py:112
  357.5 25.5 %collective-permute-start.8 = (bf16[512,768]{1,0:T(8,128)(2,1)}, bf16[512,768]{1,0:T(8,128)(2,1)}, u32[]{:S(2)}, u32[]{:S(2)}) collective-permute-start(bf16[512,768]{1,0:T(8,128)(2,1)} %get-tuple-element.47), channel_id=1, source_target_pairs={{3,2},{2,1},{7,6},{6,5},{11,10},{10,9},{15,14},{14,13},{19,18},{18... | collective-permute-start | bytes 2359304 | tf_op jit(solution)/shard_map/ppermute | solution.py:113
  359.1 23.9 %copy-start.4 = (bf16[2048,512]{1,0:T(8,128)(2,1)S(1)}, bf16[2048,512]{1,0:T(8,128)(2,1)}, u32[]{:S(2)}) copy-start(bf16[2048,512]{1,0:T(8,128)(2,1)} %copy-done.2) | copy-start | bytes 6291460
  359.1 23.9 %copy-start.8 = (bf16[2048,256]{1,0:T(8,128)(2,1)S(1)}, bf16[2048,256]{1,0:T(8,128)(2,1)}, u32[]{:S(2)}) copy-start(bf16[2048,256]{1,0:T(8,128)(2,1)} %copy-done.6) | copy-start | bytes 3145732
  369.0 30.8 %collective-permute-start.13 = (bf16[512,768]{1,0:T(8,128)(2,1)}, bf16[512,768]{1,0:T(8,128)(2,1)}, u32[]{:S(2)}, u32[]{:S(2)}) collective-permute-start(bf16[512,768]{1,0:T(8,128)(2,1)} %get-tuple-element.38), channel_id=1, source_target_pairs={{0,1},{1,2},{2,3},{4,5},{5,6},{6,7},{8,9},{9,10},{10,11},{12,13},{... | collective-permute-start | bytes 2359304 | tf_op jit(solution)/shard_map/ppermute | solution.py:112
  374.3 25.5 %collective-permute-start.16 = (bf16[512,768]{1,0:T(8,128)(2,1)}, bf16[512,768]{1,0:T(8,128)(2,1)}, u32[]{:S(2)}, u32[]{:S(2)}) collective-permute-start(bf16[512,768]{1,0:T(8,128)(2,1)} %get-tuple-element.39), channel_id=1, source_target_pairs={{3,2},{2,1},{1,0},{7,6},{6,5},{5,4},{11,10},{10,9},{9,8},{15,14},{... | collective-permute-start | bytes 2359304 | tf_op jit(solution)/shard_map/ppermute | solution.py:113
  385.9 30.7 %collective-permute-start.6 = (bf16[512,768]{1,0:T(8,128)(2,1)}, bf16[512,768]{1,0:T(8,128)(2,1)}, u32[]{:S(2)}, u32[]{:S(2)}) collective-permute-start(bf16[512,768]{1,0:T(8,128)(2,1)} %get-tuple-element.44), channel_id=1, source_target_pairs={{0,1},{1,2},{2,3},{4,5},{5,6},{6,7},{8,9},{9,10},{10,11},{12,13},{... | collective-permute-start | bytes 2359304 | tf_op jit(solution)/shard_map/ppermute | solution.py:112
  391.2 25.4 %collective-permute-start.9 = (bf16[512,768]{1,0:T(8,128)(2,1)}, bf16[512,768]{1,0:T(8,128)(2,1)}, u32[]{:S(2)}, u32[]{:S(2)}) collective-permute-start(bf16[512,768]{1,0:T(8,128)(2,1)} %get-tuple-element.45), channel_id=1, source_target_pairs={{3,2},{2,1},{1,0},{7,6},{6,5},{5,4},{11,10},{10,9},{9,8},{15,14},{... | collective-permute-start | bytes 2359304 | tf_op jit(solution)/shard_map/ppermute | solution.py:113
  403.9 12.7 %copy-start.5 = (bf16[2048,512]{1,0:T(8,128)(2,1)S(1)}, bf16[2048,512]{1,0:T(8,128)(2,1)}, u32[]{:S(2)}) copy-start(bf16[2048,512]{1,0:T(8,128)(2,1)} %copy-done.2) | copy-start | bytes 6291460
  403.9 12.7 %copy-start.9 = (bf16[2048,256]{1,0:T(8,128)(2,1)S(1)}, bf16[2048,256]{1,0:T(8,128)(2,1)}, u32[]{:S(2)}) copy-start(bf16[2048,256]{1,0:T(8,128)(2,1)} %copy-done.6) | copy-start | bytes 3145732
  (24 other events, 145.6 us)
Sparse Core Ops, SparseCore 0:
  32.8 64.9 all-gather.3
  110.1 63.9 all-gather.5
  194.1 76.7 all-gather.7
  273.1 74.0 reduce-scatter.1
